TPU v7x, 512 devices: a whole 4x4x16 slice. The times are simulated.
512 devices in a mesh: dp: 4 (over x), expert: 128 (over z, y, core).
Axes of the slice: x: 4, y: 4, z: 16, core: 2. Of those that a mesh axis runs over, the one named last changes fastest.
Arguments:
- tokens: bfloat16 [65536, 2048], P(('dp', 'expert')), may hold values from -6 to 6
- cotangent: bfloat16 [65536, 2048], P(('dp', 'expert')), may hold values from -0.59765625 to 0.59765625
- gate_values: bfloat16 [65536, 4], P(('dp', 'expert')), may hold values from 0.049804688 to 0.59765625
- expert_ids: int32 [65536, 4], P(('dp', 'expert')), may hold values from 0 to 127, all different within a row
- hot_plan: int32 [128], replicated, may hold values from 0 to 1, as said below
- expert_caps: int32 [128], replicated, may hold values from 1 to 4
- w_up: bfloat16 [128, 2048, 384], P('expert'), may hold values from -0.125 to 0.125
- w_down: bfloat16 [128, 384, 2048], P('expert'), may hold values from -0.3125 to 0.3125
Outputs:
- grad_up: bfloat16 [128, 2048, 384], P('expert', 'dp')
- grad_down: bfloat16 [128, 384, 2048], P('expert', None, 'dp')
- gate_grad: float32 [65536, 4], P(('dp', 'expert'))
Inputs may be any that keep to these rules, and one draw needn't show every extreme that they name: hot_plan holds 0 or 1; the entries of experts 0 and 126 are always 1.
All inputs are finite; a program needn't handle non-finite values.
Results may differ from a plain program's by a relative error of at most 0.013.
Values may be sent and summed in bfloat16 or wider, within the bound.
No kernel may reach another device: no remote copies, remote signals or barrier semaphores. Data moves between devices by JAX's collectives and lax.ppermute only.
A program may use at most 64 MiB of HBM per device.

v0:
```python
import jax
import jax.numpy as jnp
from jax import lax
from jax.sharding import PartitionSpec as P


def from_behind(block, axis, distance):
    devices = range(lax.axis_size(axis))
    route = [((i - distance) % len(devices), i) for i in devices]
    return lax.ppermute(block, axis, route)


def route_plan(id_flat, source, hot_plan, expert_caps, expert_count, capacity):
    expert_iota = jnp.arange(expert_count, dtype=jnp.int32)
    one_hot = (id_flat[:, None] == expert_iota[None, :]).astype(jnp.int32)
    earlier = jnp.cumsum(one_hot, axis=0) - one_hot
    expert_rank = jnp.sum(earlier * one_hot, axis=1)
    cap_of = jnp.sum(one_hot * expert_caps[None, :], axis=1)
    hot_of = jnp.sum(one_hot * hot_plan[None, :], axis=1)
    admitted = expert_rank < cap_of
    moved = (hot_of == 1) & (source % 2 == 1)
    target = jnp.where(moved, (id_flat + 1) % expert_count, id_flat)
    target_hot = (target[:, None] == expert_iota[None, :]).astype(jnp.int32)
    counted = target_hot * admitted[:, None].astype(jnp.int32)
    before = jnp.cumsum(counted, axis=0) - counted
    slot_rank = jnp.sum(before * target_hot, axis=1)
    kept_mask = admitted & (slot_rank < capacity)
    replica = target != id_flat
    return (target, slot_rank, kept_mask, replica)


def pack_slots(
    tokens, cotangent, gate_values, target, slot_rank, kept_mask, replica, expert_count, capacity
):
    count = target.shape[0]
    width_d = tokens.shape[1]
    top_count = gate_values.shape[1]
    total = expert_count * capacity
    slot = jnp.where(kept_mask, target * capacity + slot_rank, total)
    filler = (
        jnp.full((total + 1,), count, jnp.int32)
        .at[slot]
        .set(jnp.arange(count, dtype=jnp.int32))[:total]
    )
    token_row = filler // top_count
    padded_x = jnp.concatenate([tokens, jnp.zeros((1, width_d), tokens.dtype)], axis=0)
    padded_dy = jnp.concatenate([cotangent, jnp.zeros((1, width_d), cotangent.dtype)], axis=0)
    sent_x = padded_x[token_row].reshape(expert_count, capacity, width_d)
    sent_dy = padded_dy[token_row].reshape(expert_count, capacity, width_d)
    gate_flat = jnp.concatenate([gate_values.reshape(-1), jnp.zeros((1,), gate_values.dtype)])[
        filler
    ]
    rep_flat = jnp.concatenate([replica, jnp.zeros((1,), bool)])[filler]
    nothing = jnp.zeros_like(gate_flat)
    sent_gate = jnp.stack(
        [jnp.where(rep_flat, nothing, gate_flat), jnp.where(rep_flat, gate_flat, nothing)], axis=-1
    )
    return (sent_x, sent_dy, sent_gate.reshape(expert_count, capacity, 2), slot)


def expert_pass(rows, dy_rows, gate_col, up_w, down_w):
    preact = jnp.dot(rows, up_w, preferred_element_type=jnp.float32)
    sigma = jax.nn.sigmoid(preact)
    hidden = (preact * sigma).astype(jnp.bfloat16)
    expert_out = jnp.dot(hidden, down_w, preferred_element_type=jnp.float32)
    gate_dot = jnp.sum(dy_rows.astype(jnp.float32) * expert_out, axis=1)
    scaled = (gate_col.astype(jnp.float32)[:, None] * dy_rows.astype(jnp.float32)).astype(
        jnp.bfloat16
    )
    grad_down = lax.dot_general(
        hidden, scaled, (((0,), (0,)), ((), ())), preferred_element_type=jnp.float32
    )
    backprop = lax.dot_general(
        scaled, down_w, (((1,), (1,)), ((), ())), preferred_element_type=jnp.float32
    )
    grad_pre = (backprop * sigma * (1.0 + preact * (1.0 - sigma))).astype(jnp.bfloat16)
    grad_up = lax.dot_general(
        rows, grad_pre, (((0,), (0,)), ((), ())), preferred_element_type=jnp.float32
    )
    return (gate_dot, grad_up, grad_down)


def shards(tokens, cotangent, gate_values, expert_ids, hot_plan, expert_caps, w_up, w_down):
    expert_count = lax.axis_size("expert")
    source = lax.axis_index("expert")
    width_d = tokens.shape[1]
    capacity = gate_values.shape[0] * gate_values.shape[1] // expert_count
    target, slot_rank, kept_mask, replica = route_plan(
        expert_ids.reshape(-1), source, hot_plan, expert_caps, expert_count, capacity
    )
    sent_x, sent_dy, sent_gate, slot = pack_slots(
        tokens,
        cotangent,
        gate_values,
        target,
        slot_rank,
        kept_mask,
        replica,
        expert_count,
        capacity,
    )
    recv_x, recv_dy, recv_gate = (
        lax.all_to_all(sent_x, "expert", split_axis=0, concat_axis=0, tiled=True),
        lax.all_to_all(sent_dy, "expert", split_axis=0, concat_axis=0, tiled=True),
        lax.all_to_all(sent_gate, "expert", split_axis=0, concat_axis=0, tiled=True),
    )
    up_own = w_up[0]
    down_own = w_down[0]
    half_count = expert_count // 2
    odd_x = recv_x.reshape(half_count, 2, capacity, width_d)[:, 1].reshape(-1, width_d)
    odd_dy = recv_dy.reshape(half_count, 2, capacity, width_d)[:, 1].reshape(-1, width_d)
    odd_gate = recv_gate.reshape(half_count, 2, capacity, 2)[:, 1, :, 1].reshape(-1)
    own_gate = recv_gate[:, :, 0].reshape(-1)
    up_rep, down_rep = from_behind((up_own, down_own), "expert", 1)
    own_dot, own_up, own_down = expert_pass(
        recv_x.reshape(-1, width_d), recv_dy.reshape(-1, width_d), own_gate, up_own, down_own
    )
    rep_dot, rep_up, rep_down = expert_pass(odd_x, odd_dy, odd_gate, up_rep, down_rep)
    home_up, home_down = from_behind(
        (rep_up.astype(jnp.bfloat16), rep_down.astype(jnp.bfloat16)), "expert", -1
    )
    part_up = (own_up + home_up.astype(jnp.float32)).astype(jnp.bfloat16)
    part_down = (own_down + home_down.astype(jnp.float32)).astype(jnp.bfloat16)
    summed_up, summed_down = (
        lax.psum_scatter(
            part_up.astype(jnp.float32).astype(jnp.bfloat16), "dp", scatter_dimension=0, tiled=True
        ).astype(jnp.float32),
        lax.psum_scatter(
            part_down.astype(jnp.float32).astype(jnp.bfloat16),
            "dp",
            scatter_dimension=1,
            tiled=True,
        ).astype(jnp.float32),
    )
    own_value = jnp.where(own_gate > 0, own_dot, 0.0).reshape(expert_count, capacity)
    rep_value = jnp.where(odd_gate > 0, rep_dot, 0.0).reshape(half_count, 1, capacity)
    rep_full = jnp.concatenate([jnp.zeros_like(rep_value), rep_value], axis=1).reshape(
        expert_count, capacity
    )
    returned = lax.all_to_all(
        own_value + rep_full, "expert", split_axis=0, concat_axis=0, tiled=True
    )
    padded = jnp.concatenate([returned.reshape(-1), jnp.zeros((1,), returned.dtype)])
    gate_grad = padded[slot].reshape(gate_values.shape)
    return (summed_up.astype(jnp.bfloat16)[None], summed_down.astype(jnp.bfloat16)[None], gate_grad)


def solution(mesh):
    placed = (
        P(("dp", "expert"), None),
        P(("dp", "expert"), None),
        P(("dp", "expert"), None),
        P(("dp", "expert"), None),
        P(),
        P(),
        P("expert", None, None),
        P("expert", None, None),
    )
    return jax.shard_map(
        shards,
        mesh=mesh,
        in_specs=placed,
        out_specs=(P("expert", "dp", None), P("expert", None, "dp"), P(("dp", "expert"), None)),
        check_vma=False,
    )
```

profile of v0, /device:TPU:1, one launch (start us, length us, event | category | flops | bytes accessed | tf_op | source)
XLA Modules:
  0.0 411.6 jit_solution(12524027919365337154)
XLA Ops:
  11.8 2.4 scatter_custom_fusion
  14.4 3.5 gather_fusion.2
  17.9 3.5 gather_fusion.1
  22.4 20.6 %all-to-all-start.1 = ((bf16[128,4,2]{1,2,0:T(2,128)(2,1)}), bf16[128,4,2]{1,2,0:T(2,128)(2,1)S(1)}, u32[]{:S(2)}, u32[]{:S(2)}) async-start(bf16[128,4,2]{1,2,0:T(2,128)(2,1)} %copy.57), calls=%async_computation.1 | async-start | bytes 131072 | tf_op jit(solution)/shard_map/all_to_all | solution.py:105
  43.0 2.5 gather_fusion
  45.5 2.2 reshape.348
  47.7 10.0 %all-to-all-done.1 = bf16[128,4,2]{1,2,0:T(2,128)(2,1)S(1)} async-done(((bf16[128,4,2]{1,2,0:T(2,128)(2,1)}), bf16[128,4,2]{1,2,0:T(2,128)(2,1)S(1)}, u32[]{:S(2)}, u32[]{:S(2)}) %all-to-all-start.1) | async-done | bytes 2080 | tf_op jit(solution)/shard_map/all_to_all | solution.py:105
  57.8 6.2 %all-to-all-start = ((bf16[128,4,2048]{2,1,0:T(4,128)(2,1)}), bf16[128,4,2048]{2,1,0:T(4,128)(2,1)S(1)}, u32[]{:S(2)}, u32[]{:S(2)}) async-start(bf16[128,4,2048]{2,1,0:T(4,128)(2,1)} %reshape.348), calls=%async_computation | async-start | bytes 4194304 | tf_op jit(solution)/shard_map/all_to_all | solution.py:103
  64.1 3.3 gather_fusion.3
  67.4 4.1 %reshape.351 = bf16[128,4,2048]{2,1,0:T(4,128)(2,1)} reshape(bf16[512,2048]{1,0:T(8,128)(2,1)} %gather_fusion.3) | data formatting | bytes 4194304 | tf_op jit(solution)/shard_map/reshape | solution.py:49
  71.5 89.3 %all-to-all-done = bf16[128,4,2048]{2,1,0:T(4,128)(2,1)S(1)} async-done(((bf16[128,4,2048]{2,1,0:T(4,128)(2,1)}), bf16[128,4,2048]{2,1,0:T(4,128)(2,1)S(1)}, u32[]{:S(2)}, u32[]{:S(2)}) %all-to-all-start) | async-done | bytes 2097184 | tf_op jit(solution)/shard_map/all_to_all | solution.py:103
  162.2 10.1 %all-to-all-start.2 = ((bf16[128,4,2048]{2,1,0:T(4,128)(2,1)}), bf16[128,4,2048]{2,1,0:T(4,128)(2,1)S(1)}, u32[]{:S(2)}, u32[]{:S(2)}) async-start(bf16[128,4,2048]{2,1,0:T(4,128)(2,1)} %reshape.351), calls=%async_computation.2 | async-start | bytes 4194304 | tf_op jit(solution)/shard_map/all_to_all | solution.py:104
  172.3 3.5 collective-permute-start.1
  178.3 2.7 slice.49
  182.3 86.8 %all-to-all-done.2 = bf16[128,4,2048]{2,1,0:T(4,128)(2,1)S(1)} async-done(((bf16[128,4,2048]{2,1,0:T(4,128)(2,1)}), bf16[128,4,2048]{2,1,0:T(4,128)(2,1)S(1)}, u32[]{:S(2)}, u32[]{:S(2)}) %all-to-all-start.2) | async-done | bytes 2097184 | tf_op jit(solution)/shard_map/all_to_all | solution.py:104
  270.7 3.0 reshape.361
  275.8 4.7 %convolution_convert_fusion.1 = bf16[2048,384]{1,0:T(8,128)(2,1)} fusion(bf16[256,2048]{1,0:T(8,128)(2,1)S(1)} %reshape_squeeze.2, bf16[384,2048]{1,0:T(8,128)(2,1)} %collective-permute-done, f32[256,384]{1,0:T(8,128)S(1)} %fusion.49, f32[256,2048]{1,0:T(8,128)} %reshape.361, f32[256]{0:T(256)S(1)} %reshape.360), kind=kOutput, calls=%fused_computation.12 | convolution fusion | flops 808026112 | bytes 6685696 | tf_op jit(solution)/shard_map/dot_general | solution.py:77
  280.5 28.5 %collective-permute-start.2 = (bf16[2048,384]{1,0:T(8,128)(2,1)}, bf16[2048,384]{1,0:T(8,128)(2,1)}, u32[]{:S(2)}, u32[]{:S(2)}) collective-permute-start(bf16[2048,384]{1,0:T(8,128)(2,1)} %convolution_convert_fusion.1), channel_id=1, source_target_pairs={{1,0},{2,1},{3,2},{4,3},{5,4},{6,5},{7,6},{8,7},{9,8},{10,9},{11,1... | collective-permute-start | bytes 4718600 | tf_op jit(solution)/shard_map/ppermute | solution.py:10
  312.0 4.0 convert_element_type.123
  316.0 4.0 reshape.349
  320.0 3.3 fusion.38
  323.3 6.8 %fusion.8 = f32[2048,384]{1,0:T(8,128)} fusion(bf16[512,2048]{1,0:T(8,128)(2,1)} %reshape.349, bf16[512,2048]{1,0:T(8,128)(2,1)} %convert_element_type.123, f32[512,384]{1,0:T(8,128)S(1)} %fusion.38, bf16[1,384,2048]{2,1,0:T(8,128)(2,1)} %param.15), kind=kOutput, calls=%fused_computation.26 | convolution fusion | flops 1612382208 | bytes 9699328 | tf_op jit(solution)/shard_map/dot_general | solution.py:77
  330.1 3.8 add_convert_fusion.1
  334.0 3.5 convolution_convert_fusion
  339.7 2.5 reshape.363
  342.2 17.6 %collective-permute-done.3 = bf16[384,2048]{1,0:T(8,128)(2,1)} collective-permute-done((bf16[384,2048]{1,0:T(8,128)(2,1)}, bf16[384,2048]{1,0:T(8,128)(2,1)}, u32[]{:S(2)}, u32[]{:S(2)}) %collective-permute-start.3) | collective-permute-done | bytes 1572896 | tf_op jit(solution)/shard_map/ppermute | solution.py:10
  359.8 5.1 %add_convert_fusion = bf16[384,2048]{1,0:T(8,128)(2,1)} fusion(bf16[384,2048]{1,0:T(8,128)(2,1)} %collective-permute-done.3, f32[512,2048]{1,0:T(8,128)} %reshape.363, f32[512]{0:T(512)S(1)} %reshape.362, f32[512,384]{1,0:T(8,128)S(1)} %fusion.38), kind=kOutput, calls=%fused_computation.9 | convolution fusion | flops 810745856 | bytes 8128512 | tf_op jit(solution)/shard_map/dot_general | solution.py:70
  364.9 2.2 fusion.2
  367.5 4.1 multiply_reduce_fusion
  372.3 13.1 %all-to-all-start.3 = ((f32[128,1,4]{2,1,0:T(1,128)}), f32[128,1,4]{2,1,0:T(1,128)S(1)}, u32[]{:S(2)}, u32[]{:S(2)}) async-start(f32[128,1,4]{2,1,0:T(1,128)} %bitcast.21), calls=%async_computation.5 | async-start | bytes 131072 | tf_op jit(solution)/shard_map/all_to_all | solution.py:140
  385.5 14.8 %all-to-all-done.3 = f32[128,1,4]{2,1,0:T(1,128)S(1)} async-done(((f32[128,1,4]{2,1,0:T(1,128)}), f32[128,1,4]{2,1,0:T(1,128)S(1)}, u32[]{:S(2)}, u32[]{:S(2)}) %all-to-all-start.3) | async-done | bytes 2080 | tf_op jit(solution)/shard_map/all_to_all | solution.py:140
  401.7 2.3 gather_fusion.4
  (89 shorter events, 23.1 us)
Async XLA Ops:
  9.7 33.3 %copy-start.4 = (bf16[128,2048]{1,0:T(8,128)(2,1)S(1)}, bf16[128,2048]{1,0:T(8,128)(2,1)}, u32[]{:S(2)}) copy-start(bf16[128,2048]{1,0:T(8,128)(2,1)} %param.8) | copy-start | bytes 1572868
  22.4 35.4 %all-to-all-start.1 = ((bf16[128,4,2]{1,2,0:T(2,128)(2,1)}), bf16[128,4,2]{1,2,0:T(2,128)(2,1)S(1)}, u32[]{:S(2)}, u32[]{:S(2)}) async-start(bf16[128,4,2]{1,2,0:T(2,128)(2,1)} %copy.57), calls=%async_computation.1 | async-start | bytes 131072 | tf_op jit(solution)/shard_map/all_to_all | solution.py:105
  47.7 16.3 %copy-start.5 = (bf16[128,2048]{1,0:T(8,128)(2,1)S(1)}, bf16[128,2048]{1,0:T(8,128)(2,1)}, u32[]{:S(2)}) copy-start(bf16[128,2048]{1,0:T(8,128)(2,1)} %param.9) | copy-start | bytes 1572868
  57.8 120.2 %copy-start.2 = (bf16[128,4,2]{1,2,0:T(2,128)(2,1)}, bf16[128,4,2]{1,2,0:T(2,128)(2,1)S(1)}, u32[]{:S(2)}) copy-start(bf16[128,4,2]{1,2,0:T(2,128)(2,1)S(1)} %all-to-all-done.1) | copy-start | bytes 6148
  57.8 103.1 %all-to-all-start = ((bf16[128,4,2048]{2,1,0:T(4,128)(2,1)}), bf16[128,4,2048]{2,1,0:T(4,128)(2,1)S(1)}, u32[]{:S(2)}, u32[]{:S(2)}) async-start(bf16[128,4,2048]{2,1,0:T(4,128)(2,1)} %reshape.348), calls=%async_computation | async-start | bytes 4194304 | tf_op jit(solution)/shard_map/all_to_all | solution.py:103
  160.9 1.4 copy-start
  162.2 107.0 %all-to-all-start.2 = ((bf16[128,4,2048]{2,1,0:T(4,128)(2,1)}), bf16[128,4,2048]{2,1,0:T(4,128)(2,1)S(1)}, u32[]{:S(2)}, u32[]{:S(2)}) async-start(bf16[128,4,2048]{2,1,0:T(4,128)(2,1)} %reshape.351), calls=%async_computation.2 | async-start | bytes 4194304 | tf_op jit(solution)/shard_map/all_to_all | solution.py:104
  172.3 232.5 %reduce-scatter.3.cloned.1.call-start = ((), (), s32[]{:S(2)}) async-start(), calls=%async_computation.6 | async-start | bytes 1966080 | tf_op jit(solution)/shard_map/reduce_scatter | solution.py:125
  172.3 101.3 %collective-permute-start.1 = (bf16[2048,384]{1,0:T(8,128)(2,1)}, bf16[2048,384]{1,0:T(8,128)(2,1)}, u32[]{:S(2)}, u32[]{:S(2)}) collective-permute-start(bf16[2048,384]{1,0:T(8,128)(2,1)} %bitcast.91), channel_id=1, source_target_pairs={{127,0},{0,1},{1,2},{2,3},{3,4},{4,5},{5,6},{6,7},{7,8},{8,9},{9,1... | collective-permute-start | bytes 4718600 | tf_op jit(solution)/shard_map/ppermute | solution.py:10
  175.9 99.9 %collective-permute-start = (bf16[384,2048]{1,0:T(8,128)(2,1)}, bf16[384,2048]{1,0:T(8,128)(2,1)}, u32[]{:S(2)}, u32[]{:S(2)}) collective-permute-start(bf16[384,2048]{1,0:T(8,128)(2,1)} %bitcast.92), channel_id=1, source_target_pairs={{127,0},{0,1},{1,2},{2,3},{3,4},{4,5},{5,6},{6,7},{7,8},{8,9},{9,1... | collective-permute-start | bytes 4718600 | tf_op jit(solution)/shard_map/ppermute | solution.py:10
  280.5 49.6 %collective-permute-start.2 = (bf16[2048,384]{1,0:T(8,128)(2,1)}, bf16[2048,384]{1,0:T(8,128)(2,1)}, u32[]{:S(2)}, u32[]{:S(2)}) collective-permute-start(bf16[2048,384]{1,0:T(8,128)(2,1)} %convolution_convert_fusion.1), channel_id=1, source_target_pairs={{1,0},{2,1},{3,2},{4,3},{5,4},{6,5},{7,6},{8,7},{9,8},{10,9},{11,1... | collective-permute-start | bytes 4718600 | tf_op jit(solution)/shard_map/ppermute | solution.py:10
  333.9 70.9 %reduce-scatter.5.cloned.1.call-start = ((), (), s32[]{:S(2)}) async-start(), calls=%async_computation.7 | async-start | bytes 1966080 | tf_op jit(solution)/shard_map/reduce_scatter | solution.py:128
  337.5 22.3 %collective-permute-start.3 = (bf16[384,2048]{1,0:T(8,128)(2,1)}, bf16[384,2048]{1,0:T(8,128)(2,1)}, u32[]{:S(2)}, u32[]{:S(2)}) collective-permute-start(bf16[384,2048]{1,0:T(8,128)(2,1)} %convolution_convert_fusion), channel_id=1, source_target_pairs={{1,0},{2,1},{3,2},{4,3},{5,4},{6,5},{7,6},{8,7},{9,8},{10,9},{11,1... | collective-permute-start | bytes 4718600 | tf_op jit(solution)/shard_map/ppermute | solution.py:10
  342.2 22.7 %copy-start.1 = (f32[256,2048]{1,0:T(8,128)S(1)}, f32[256,2048]{1,0:T(8,128)}, u32[]{:S(2)}) copy-start(f32[256,2048]{1,0:T(8,128)} %reshape.361) | copy-start | bytes 6291460
  367.4 4.2 %copy-start.3 = (bf16[128,4,2]{1,2,0:T(2,128)(2,1)S(1)}, bf16[128,4,2]{1,2,0:T(2,128)(2,1)}, u32[]{:S(2)}) copy-start(bf16[128,4,2]{1,2,0:T(2,128)(2,1)} %copy-done.2) | copy-start | bytes 6148
  372.3 28.0 %all-to-all-start.3 = ((f32[128,1,4]{2,1,0:T(1,128)}), f32[128,1,4]{2,1,0:T(1,128)S(1)}, u32[]{:S(2)}, u32[]{:S(2)}) async-start(f32[128,1,4]{2,1,0:T(1,128)} %bitcast.21), calls=%async_computation.5 | async-start | bytes 131072 | tf_op jit(solution)/shard_map/all_to_all | solution.py:140
Sparse Core Ops, SparseCore 0:
  334.0 28.1 reduce-scatter.2
  365.7 33.1 reduce-scatter.4
where the time goes:
time: 413 us; the launch traced here: 412 us
  waiting for transfers between devices  219 us (53%)
  starting transfers between devices  86.3 us (21%)
  local copies, waits for them, and re-layouts  48.4 us (12%)
  matrix products  31.7 us (8%)
  between operations  14.5 us (4%)
  other arithmetic  12 us (3%)
    all_to_all x1, waiting for transfers between devices, shards(): lax.all_to_all(sent_x, 'expert', split_axis=0, concat_axis=0, tiled=True)  89.3 us
    all_to_all x1, waiting for transfers between devices, shards(): lax.all_to_all(sent_dy, 'expert', split_axis=0, concat_axis=0, tiled=True)  86.8 us
    ppermute x4, starting transfers between devices, from_behind(): return lax.ppermute(block, axis, route)  36.2 us
    all_to_all x1, starting transfers between devices, shards(): lax.all_to_all(sent_gate, 'expert', split_axis=0, concat_axis=0, tiled=True)  20.6 us
    ppermute x4, waiting for transfers between devices, from_behind(): return lax.ppermute(block, axis, route)  17.6 us
    all_to_all x1, waiting for transfers between devices, shards(): lax.all_to_all(own_value + rep_full, 'expert', split_axis=0, concat_axis=...  14.8 us
    all_to_all x1, starting transfers between devices, shards(): lax.all_to_all(own_value + rep_full, 'expert', split_axis=0, concat_axis=...  13.1 us
    dot_general x2, matrix products, expert_pass(): lax.dot_general(rows, grad_pre, (((0,), (0,)), ((), ())), preferred_eleme...  11.5 us
  transfers between devices with their start and end apart: 10, of which 5 were waited for; matrix products, arithmetic and copies ran while one was open for 16% of the time, Pallas kernels for 0%

commit v1 on v0

v1 whole, which is shorter than its diff:
```python
import functools

import jax
import jax.numpy as jnp
from jax import lax
from jax.experimental import pallas as pl
from jax.experimental.pallas import tpu as pltpu
from jax.sharding import PartitionSpec as P

SLOTS = 4
CHUNK = 2 * SLOTS


def contract(a, b, dims):
    return lax.dot_general(a, b, (dims, ((), ())), preferred_element_type=jnp.float32)


def route_pack(odd_ref, ids_ref, gates_ref, hot_ref, caps_ref, x_ref, dy_ref, sent_ref, code_ref):
    count = ids_ref.shape[0]
    experts = hot_ref.shape[1]
    wide = experts * CHUNK
    lane = lax.broadcasted_iota(jnp.int32, (count, experts), 1)
    row = lax.broadcasted_iota(jnp.int32, (count, count), 0)
    col = lax.broadcasted_iota(jnp.int32, (count, count), 1)
    below = (col < row).astype(jnp.bfloat16)
    picked = jnp.zeros((count, experts), jnp.float32)
    place = jnp.zeros((count, experts), jnp.float32)
    gate = jnp.zeros((count, experts), jnp.float32)
    for k in range(ids_ref.shape[1]):
        hit = ids_ref[:, k : k + 1] == lane
        picked = jnp.where(hit, 1.0, picked)
        place = jnp.where(hit, float(k), place)
        gate = jnp.where(hit, gates_ref[:, k : k + 1].astype(jnp.float32), gate)
    rank = contract(below, picked.astype(jnp.bfloat16), ((1,), (0,)))
    admitted = jnp.where(rank < caps_ref[...].astype(jnp.float32), picked, 0.0)
    moves = hot_ref[...].astype(jnp.float32) * odd_ref[0].astype(jnp.float32)
    moved = admitted * moves
    stay = admitted - moved
    moved_next = pltpu.roll(moved, 1, 1)
    stay_next = pltpu.roll(stay, experts - 1, 1)
    before = contract(below, (stay + moved_next).astype(jnp.bfloat16), ((1,), (0,)))
    tie_stay = jnp.where(pltpu.roll(place, 1, 1) < place, moved_next, 0.0)
    tie_move = jnp.where(pltpu.roll(place, experts - 1, 1) < place, stay_next, 0.0)
    slot = jnp.where(moves > 0, pltpu.roll(before, experts - 1, 1) + tie_move, before + tie_stay)
    code = jnp.where((admitted > 0) & (slot < SLOTS), rank, -8.0)
    code_ref[...] = code
    spread = (
        lax.broadcasted_iota(jnp.int32, (experts, wide), 1) // CHUNK
        == lax.broadcasted_iota(jnp.int32, (experts, wide), 0)
    ).astype(jnp.bfloat16)
    part = lax.broadcasted_iota(jnp.int32, (count, wide), 1) % CHUNK
    code_wide = contract(code.astype(jnp.bfloat16), spread, ((1,), (0,)))
    gate_wide = contract(gate.astype(jnp.bfloat16), spread, ((1,), (0,)))
    take_x = (code_wide == part.astype(jnp.float32)).astype(jnp.bfloat16)
    chosen = code_wide == (part - SLOTS).astype(jnp.float32)
    take_dy = chosen.astype(jnp.bfloat16)
    gate_pick = jnp.where(chosen, gate_wide, 0.0).astype(jnp.bfloat16)
    ones = jnp.ones((count, 128), jnp.bfloat16)
    gate_col = contract(gate_pick, ones, ((0,), (0,)))
    gate_col = jnp.concatenate([gate_col] * 4, axis=1)
    step = gate_col.shape[1]
    for c in range(x_ref.shape[1] // step):
        at = slice(c * step, (c + 1) * step)
        rows_x = contract(take_x, x_ref[:, at], ((0,), (0,)))
        rows_dy = contract(take_dy, dy_ref[:, at], ((0,), (0,)))
        sent_ref[:, at] = (rows_x + gate_col * rows_dy).astype(jnp.bfloat16)


def expert_grads(recv_ref, up_ref, down_ref, grad_up_ref, grad_down_ref, dot_ref, hid_ref, pre_ref):
    total, width = recv_ref.shape
    hidden_width = up_ref.shape[1]
    step = min(256, total)
    for r in range(total // step):
        at = slice(r * step, (r + 1) * step)
        block = recv_ref[at, :]
        preact = contract(block, up_ref[...], ((1,), (0,)))
        backprop = contract(block, down_ref[...], ((1,), (1,)))
        backprop = pltpu.roll(backprop, step - SLOTS, 0)
        lower = lax.broadcasted_iota(jnp.int32, (step, hidden_width), 0) % CHUNK < SLOTS
        sigma = jax.nn.sigmoid(preact)
        hidden = jnp.where(lower, preact * sigma, 0.0).astype(jnp.bfloat16).astype(jnp.float32)
        grad_pre = backprop * sigma * (1.0 + preact * (1.0 - sigma))
        pre_ref[at, :] = jnp.where(lower, grad_pre, 0.0).astype(jnp.bfloat16)
        hid_ref[at, :] = pltpu.roll(hidden, SLOTS, 0).astype(jnp.bfloat16)
        dots = jnp.sum(hidden * backprop, axis=1, keepdims=True)
        lane = lax.broadcasted_iota(jnp.int32, (step, 128), 1)
        sub = lax.broadcasted_iota(jnp.int32, (step, 128), 0) % CHUNK
        spread = jnp.where(lane == sub, dots, 0.0).reshape(step // CHUNK, CHUNK, 128)
        dot_ref[r * (step // CHUNK) : (r + 1) * (step // CHUNK), :] = jnp.sum(spread, axis=1)
    wide = min(512, width)
    for c in range(width // wide):
        at = slice(c * wide, (c + 1) * wide)
        grad_up_ref[at, :] = contract(recv_ref[:, at], pre_ref[...], ((0,), (0,))).astype(jnp.bfloat16)
        grad_down_ref[:, at] = contract(hid_ref[...], recv_ref[:, at], ((0,), (0,))).astype(jnp.bfloat16)


def gate_back(back_ref, code_ref, ids_ref, gates_ref, out_ref):
    count, experts = code_ref.shape
    back = back_ref[...].T
    code = code_ref[...]
    value = jnp.zeros((count, experts), jnp.float32)
    for j in range(SLOTS):
        value = jnp.where(code == float(j), back[j : j + 1, :], value)
    lane = lax.broadcasted_iota(jnp.int32, (count, experts), 1)
    for k in range(ids_ref.shape[1]):
        hit = ids_ref[:, k : k + 1] == lane
        total = jnp.sum(jnp.where(hit, value, 0.0), axis=1, keepdims=True)
        out_ref[:, k : k + 1] = total / gates_ref[:, k : k + 1].astype(jnp.float32)


VMEM = pl.BlockSpec(memory_space=pltpu.VMEM)
SMEM = pl.BlockSpec(memory_space=pltpu.SMEM)


def shards(tokens, cotangent, gate_values, expert_ids, hot_plan, expert_caps, w_up, w_down):
    experts = lax.axis_size("expert")
    count, width = tokens.shape
    hidden_width = w_up.shape[2]
    odd = (lax.axis_index("expert") % 2).astype(jnp.int32).reshape(1)
    sent, code = pl.pallas_call(
        route_pack,
        out_shape=(
            jax.ShapeDtypeStruct((experts * CHUNK, width), jnp.bfloat16),
            jax.ShapeDtypeStruct((count, experts), jnp.float32),
        ),
        in_specs=[SMEM] + [VMEM] * 6,
        out_specs=(VMEM, VMEM),
        compiler_params=pltpu.CompilerParams(vmem_limit_bytes=48 << 20),
    )(odd, expert_ids, gate_values, hot_plan.reshape(1, -1), expert_caps.reshape(1, -1), tokens, cotangent)
    recv = lax.all_to_all(
        sent.reshape(experts, CHUNK, width), "expert", split_axis=0, concat_axis=0, tiled=True
    )
    grad_up, grad_down, dots = pl.pallas_call(
        expert_grads,
        out_shape=(
            jax.ShapeDtypeStruct((width, hidden_width), jnp.bfloat16),
            jax.ShapeDtypeStruct((hidden_width, width), jnp.bfloat16),
            jax.ShapeDtypeStruct((experts, 128), jnp.float32),
        ),
        in_specs=[VMEM] * 3,
        out_specs=(VMEM,) * 3,
        scratch_shapes=[
            pltpu.VMEM((experts * CHUNK, hidden_width), jnp.bfloat16),
            pltpu.VMEM((experts * CHUNK, hidden_width), jnp.bfloat16),
        ],
        compiler_params=pltpu.CompilerParams(vmem_limit_bytes=48 << 20),
    )(recv.reshape(experts * CHUNK, width), w_up[0], w_down[0])
    summed_up = lax.psum_scatter(grad_up, "dp", scatter_dimension=0, tiled=True)
    summed_down = lax.psum_scatter(grad_down, "dp", scatter_dimension=1, tiled=True)
    back = lax.all_to_all(
        dots.reshape(experts, 1, 128), "expert", split_axis=0, concat_axis=0, tiled=True
    )
    gate_grad = pl.pallas_call(
        gate_back,
        out_shape=jax.ShapeDtypeStruct(gate_values.shape, jnp.float32),
        in_specs=[VMEM] * 4,
        out_specs=VMEM,
    )(back.reshape(experts, 128), code, expert_ids, gate_values)
    return summed_up[None], summed_down[None], gate_grad


def solution(mesh):
    rows = P(("dp", "expert"), None)
    return jax.shard_map(
        shards,
        mesh=mesh,
        in_specs=(rows, rows, rows, rows, P(), P(), P("expert", None, None), P("expert", None, None)),
        out_specs=(P("expert", "dp", None), P("expert", None, "dp"), rows),
        check_vma=False,
    )
```

time: 413 us -> 307 us (0.74)
  blocking collectives: 0 us -> 232 us
  waiting for transfers between devices: 219 us -> 35.5 us
  starting transfers between devices: 86.3 us -> 0.08 us
  local copies, waits for them, and re-layouts: 48.4 us -> 6.53 us
  matrix products: 31.7 us -> 0 us
  Pallas kernels: 0 us -> 18 us
  other arithmetic: 12 us -> 0 us
    all_to_all x0 -> x2, blocking collectives: none -> 232 us  [the longest x1 204 us: shards(): lax.all_to_all(sent.reshape(experts, CHUNK, width), 'expert', split_axis=...]
    all_to_all x4 -> x0, waiting for transfers between devices: 201 us -> none  [the longest x1 89.3 us: shards(): lax.all_to_all(sent_x, 'expert', split_axis=0, concat_axis=0, tiled=True)]
    all_to_all x4 -> x0, starting transfers between devices: 50 us -> none  [the longest x1 20.6 us: shards(): lax.all_to_all(sent_gate, 'expert', split_axis=0, concat_axis=0, tiled=True)]
    ppermute x4 -> x0, starting transfers between devices: 36.2 us -> none  [from_behind(): return lax.ppermute(block, axis, route)]
    reduce_scatter x2, waiting for transfers between devices: 0.01 us -> 34.8 us  [the longest x1 34.8 us: shards(): lax.psum_scatter(grad_down, 'dp', scatter_dimension=1, tiled=True)]
    dot_general x8 -> x0, matrix products: 31.7 us -> none  [the longest x2 11.5 us: expert_pass(): lax.dot_general(rows, grad_pre, (((0,), (0,)), ((), ())), preferred_eleme...]
    pallas_call x0 -> x3, Pallas kernels: none -> 18 us  [the longest x1 12.8 us: shards(): pl.pallas_call(expert_grads, out_shape=(jax.ShapeDtypeStruct((width, hidd...]
    ppermute x4 -> x0, waiting for transfers between devices: 17.6 us -> none  [from_behind(): return lax.ppermute(block, axis, route)]
  transfers between devices with their start and end apart: 10 -> 2, of which waited for: 5 -> 1; matrix products, arithmetic and copies ran while one was open for 16% -> 0% of each run, Pallas kernels for 0% -> 1%
where the time goes in v1:
time: 307 us
  blocking collectives  232 us (76%)
  waiting for transfers between devices  35.5 us (12%)
  Pallas kernels  18 us (6%)
  between operations  14.1 us (5%)
  local copies, waits for them, and re-layouts  6.53 us (2%)
    all_to_all x1, blocking collectives, shards(): lax.all_to_all(sent.reshape(experts, CHUNK, width), 'expert', split_axis=...  204 us
    reduce_scatter x1, waiting for transfers between devices, shards(): lax.psum_scatter(grad_down, 'dp', scatter_dimension=1, tiled=True)  34.8 us
    all_to_all x1, blocking collectives, shards(): lax.all_to_all(dots.reshape(experts, 1, 128), 'expert', split_axis=0, con...  27.9 us
    pallas_call x1, Pallas kernels, shards(): pl.pallas_call(expert_grads, out_shape=(jax.ShapeDtypeStruct((width, hidd...  12.8 us
    unnamed x19, local copies, waits for them, and re-layouts  6.53 us
  transfers between devices with their start and end apart: 2, of which 1 were waited for; matrix products, arithmetic and copies ran while one was open for 0% of the time, Pallas kernels for 1%

profile of v1, /device:TPU:1, one launch (start us, length us, event | category | flops | bytes accessed | tf_op | source)
XLA Modules:
  0.0 306.7 jit_solution(9056422955711130124)
XLA Ops:
  7.2 0.0 reduce-scatter.3.cloned.1.call-start
  7.2 0.8 copy.17.gates_ref
  8.0 0.0 copy-start.4
  8.0 0.8 copy.16.ids_ref
  8.8 0.0 copy-start.1
  8.8 0.0 copy-start.2
  8.9 1.1 copy-done.2
  9.9 0.0 copy-start.3
  9.9 1.0 copy-done.3
  11.0 0.0 copy-start.6
  11.0 0.7 copy-done.6
  11.6 0.0 copy-start.7
  11.6 0.7 copy-done.7
  12.3 3.2 %shard_map.103 = (bf16[1024,2048]{1,0:T(8,128)(2,1)S(1)}, f32[128,128]{1,0:T(8,128)S(1)}) custom-call(s32[1]{0:T(128)} %bitcast.odd_ref, s32[128,4]{1,0:T(8,128)S(1)} %copy.16.ids_ref, bf16[128,4]{1,0:T(8,128)(2,1)S(1)} %copy.17.gates_ref, s32[1,128]{1,0:T(1,128)S(1)} %bitcast.16, s32[1,128]{1,0:T(1,128)S(1)} %bitcast.17, bf16[128,2048]{1,0:T(8,128)(2,1)S(1)} %copy-done.2, ...), custom_call_target="tpu_custom_call" | custom-call | tf_op jit(solution)/shard_map/pallas_call | solution.py:120
  15.5 0.0 copy-start.5
  15.5 0.0 copy-start
  15.5 204.5 %all_to_all.10 = bf16[128,8,2048]{2,1,0:T(8,128)(2,1)} all-to-all(bf16[128,8,2048]{2,1,0:T(8,128)(2,1)S(1)} %bitcast.13), channel_id=1, replica_groups=mesh['dp'=4,'expert'=128] {'expert'}, dimensions={0} | all-to-all | bytes 8388608 | tf_op jit(solution)/shard_map/all_to_all | solution.py:130
  220.0 0.0 copy-done.4
  220.0 0.0 copy-done.1
  220.0 0.0 copy-done.5
  220.0 0.0 copy-done
  220.0 12.8 %shard_map.104 = (bf16[2048,384]{1,0:T(8,128)(2,1)}, bf16[384,2048]{1,0:T(8,128)(2,1)}, f32[128,128]{1,0:T(8,128)S(1)}) custom-call(bf16[1024,2048]{1,0:T(8,128)(2,1)} %bitcast.18, bf16[2048,384]{1,0:T(8,128)(2,1)S(1)} %bitcast.14, bf16[384,2048]{1,0:T(8,128)(2,1)} %bitcast.19), custom_call_target="tpu_custom_call" | custom-call | tf_op jit(solution)/shard_map/pallas_call | solution.py:133
  232.8 0.0 reduce-scatter.3.cloned.1.call-update
  232.9 0.0 reduce-scatter.5.cloned.1.call-start
  232.9 0.7 reduce-scatter.5.cloned.1.call-update
  233.6 27.9 %all_to_all.11 = f32[128,1,128]{2,1,0:T(1,128)} all-to-all(f32[128,1,128]{2,1,0:T(1,128)S(1)} %bitcast.15), channel_id=1, replica_groups=mesh['dp'=4,'expert'=128] {'expert'}, dimensions={0} | all-to-all | bytes 131072 | tf_op jit(solution)/shard_map/all_to_all | solution.py:150
  261.5 2.0 shard_map.105
  263.5 1.5 copy.21
  265.0 0.0 reduce-scatter.3.cloned.1.call-done
  265.0 34.8 %reduce-scatter.5.cloned.1.call-done = bf16[384,512]{1,0:T(8,128)(2,1)} async-done(((bf16[384,2048]{1,0:T(8,128)(2,1)}), bf16[384,512]{1,0:T(8,128)(2,1)}) %reduce-scatter.5.cloned.1.call-update) | async-done | bytes 393232 | tf_op jit(solution)/shard_map/reduce_scatter | solution.py:149
Async XLA Ops:
  7.2 257.8 %reduce-scatter.3.cloned.1.call-start = ((), (), s32[]{:S(2)}) async-start(), calls=%async_computation.4 | async-start | bytes 1966080 | tf_op jit(solution)/shard_map/reduce_scatter | solution.py:148
  8.0 212.0 %copy-start.4 = (bf16[128,4]{1,0:T(8,128)(2,1)}, bf16[128,4]{1,0:T(8,128)(2,1)S(1)}, u32[]{:S(2)}) copy-start(bf16[128,4]{1,0:T(8,128)(2,1)S(1)} %copy.17.gates_ref) | copy-start | bytes 3076
  8.8 211.2 %copy-start.1 = (s32[128,4]{1,0:T(8,128)}, s32[128,4]{1,0:T(8,128)S(1)}, u32[]{:S(2)}) copy-start(s32[128,4]{1,0:T(8,128)S(1)} %copy.16.ids_ref) | copy-start | bytes 6148
  8.8 1.1 copy-start.2
  9.9 1.0 copy-start.3
  11.0 0.7 copy-start.6
  11.6 0.7 copy-start.7
  15.5 204.5 %copy-start.5 = (f32[128,128]{1,0:T(8,128)}, f32[128,128]{1,0:T(8,128)S(1)}, u32[]{:S(2)}) copy-start(f32[128,128]{1,0:T(8,128)S(1)} %get-tuple-element.12.code_ref) | copy-start | bytes 196612
  15.5 204.5 %copy-start = (bf16[1,2048,384]{2,1,0:T(8,128)(2,1)S(1)}, bf16[1,2048,384]{2,1,0:T(8,128)(2,1)}, u32[]{:S(2)}) copy-start(bf16[1,2048,384]{2,1,0:T(8,128)(2,1)} %param.14) | copy-start | bytes 4718596
  232.9 67.0 %reduce-scatter.5.cloned.1.call-start = ((), (), s32[]{:S(2)}) async-start(), calls=%async_computation.5 | async-start | bytes 1966080 | tf_op jit(solution)/shard_map/reduce_scatter | solution.py:149
Sparse Core Ops, SparseCore 0:
  233.0 30.2 reduce-scatter.2
  266.7 33.0 reduce-scatter.4

commit v2 on v1

v2 whole, which is shorter than its diff:
```python
import jax
import jax.numpy as jnp
from jax import lax
from jax.experimental import pallas as pl
from jax.experimental.pallas import tpu as pltpu
from jax.sharding import PartitionSpec as P

SLOTS = 4
CHUNK = 2 * SLOTS
LANES = 128


def contract(a, b, dims):
    return lax.dot_general(a, b, (dims, ((), ())), preferred_element_type=jnp.float32)


def route_pack(
    odd_ref, ids_hbm, gates_hbm, hot_hbm, caps_hbm, x_hbm, dy_hbm, sent_hbm, code_ref,
    ids_ref, gates_ref, hot_ref, caps_ref, x_ref, dy_ref, sent_ref, sems,
):
    pairs = (
        (ids_hbm, ids_ref), (gates_hbm, gates_ref), (hot_hbm, hot_ref),
        (caps_hbm, caps_ref), (x_hbm, x_ref), (dy_hbm, dy_ref),
    )
    copies = [pltpu.make_async_copy(a, b, sems.at[i]) for i, (a, b) in enumerate(pairs)]
    for copy in copies:
        copy.start()
    top, count = ids_ref.shape
    experts = hot_ref.shape[1]
    wide = experts * CHUNK
    lane = lax.broadcasted_iota(jnp.int32, (count, experts), 1).astype(jnp.float32)
    row = lax.broadcasted_iota(jnp.int32, (count, count), 0)
    col = lax.broadcasted_iota(jnp.int32, (count, count), 1)
    below = (col < row).astype(jnp.bfloat16)
    eye = (col == row).astype(jnp.bfloat16)
    each = (
        lax.broadcasted_iota(jnp.int32, (top, top * experts), 1) // experts
        == lax.broadcasted_iota(jnp.int32, (top, top * experts), 0)
    ).astype(jnp.bfloat16)
    spread = (
        lax.broadcasted_iota(jnp.int32, (experts, wide), 1) // CHUNK
        == lax.broadcasted_iota(jnp.int32, (experts, wide), 0)
    ).astype(jnp.bfloat16)
    for copy in copies[:4]:
        copy.wait()
    ids = contract(ids_ref[...].astype(jnp.bfloat16), each, ((0,), (0,)))
    gates = contract(gates_ref[...], each, ((0,), (0,)))
    picked = jnp.zeros((count, experts), jnp.float32)
    place = jnp.zeros((count, experts), jnp.float32)
    gate = jnp.zeros((count, experts), jnp.float32)
    for k in range(top):
        at = slice(k * experts, (k + 1) * experts)
        hit = ids[:, at] == lane
        picked = jnp.where(hit, 1.0, picked)
        place = jnp.where(hit, float(k), place)
        gate = jnp.where(hit, gates[:, at], gate)
    rank = contract(below, picked.astype(jnp.bfloat16), ((1,), (0,)))
    admitted = jnp.where(rank < caps_ref[...].astype(jnp.float32), picked, 0.0)
    moves = hot_ref[...].astype(jnp.float32) * odd_ref[0].astype(jnp.float32)
    moved = admitted * moves
    stay = admitted - moved
    moved_next = pltpu.roll(moved, 1, 1)
    stay_next = pltpu.roll(stay, experts - 1, 1)
    before = contract(below, (stay + moved_next).astype(jnp.bfloat16), ((1,), (0,)))
    tie_stay = jnp.where(pltpu.roll(place, 1, 1) < place, moved_next, 0.0)
    tie_move = jnp.where(pltpu.roll(place, experts - 1, 1) < place, stay_next, 0.0)
    slot = jnp.where(moves > 0, pltpu.roll(before, experts - 1, 1) + tie_move, before + tie_stay)
    code = jnp.where((admitted > 0) & (slot < SLOTS), rank, -8.0).astype(jnp.bfloat16)
    code_ref[...] = contract(code, eye, ((0,), (0,)))
    part = lax.broadcasted_iota(jnp.int32, (count, wide), 1) % CHUNK
    code_wide = contract(code, spread, ((1,), (0,)))
    gate_wide = contract(gate.astype(jnp.bfloat16), spread, ((1,), (0,)))
    take_x = (code_wide == part.astype(jnp.float32)).astype(jnp.bfloat16)
    chosen = code_wide == (part - SLOTS).astype(jnp.float32)
    take_dy = chosen.astype(jnp.bfloat16)
    gate_pick = jnp.where(chosen, gate_wide, 0.0).astype(jnp.bfloat16)
    ones = jnp.ones((count, LANES), jnp.bfloat16)
    gate_col = contract(gate_pick, ones, ((0,), (0,)))
    gate_col = jnp.concatenate([gate_col] * 4, axis=1)
    step = gate_col.shape[1]
    for copy in copies[4:]:
        copy.wait()
    for c in range(x_ref.shape[1] // step):
        at = slice(c * step, (c + 1) * step)
        rows_x = contract(take_x, x_ref[:, at], ((0,), (0,)))
        rows_dy = contract(take_dy, dy_ref[:, at], ((0,), (0,)))
        sent_ref[:, at] = (rows_x + gate_col * rows_dy).astype(jnp.bfloat16)
        copies.append(pltpu.make_async_copy(sent_ref.at[:, at], sent_hbm.at[:, at], sems.at[6 + c]))
        copies[-1].start()
    for copy in copies[6:]:
        copy.wait()


def expert_down(
    recv_ref, up_ref, down_ref, grad_ref, dot_ref, x_ref, pre_ref, s_ref, hid_ref
):
    half, width = x_ref.shape
    step = half // 4
    lower = lax.broadcasted_iota(jnp.int32, (step, width), 0) % CHUNK < SLOTS
    lane = lax.broadcasted_iota(jnp.int32, (step, LANES), 1)
    sub = lax.broadcasted_iota(jnp.int32, (step, LANES), 0) % CHUNK
    for r in range(4):
        at = slice(r * step, (r + 1) * step)
        first = recv_ref[at, :]
        second = recv_ref[r * step + half : (r + 1) * step + half, :]
        x = jnp.where(lower, first, pltpu.roll(second, SLOTS, 0))
        s = jnp.where(lower, pltpu.roll(first, step - SLOTS, 0), second)
        x_ref[at, :] = x
        s_ref[at, :] = s
        preact = contract(x, up_ref[...], ((1,), (0,)))
        backprop = contract(s, down_ref[...], ((1,), (1,)))
        sigma = jax.nn.sigmoid(preact)
        hidden = (preact * sigma).astype(jnp.bfloat16)
        hid_ref[at, :] = hidden
        pre_ref[at, :] = (backprop * sigma * (1.0 + preact * (1.0 - sigma))).astype(jnp.bfloat16)
        dots = jnp.sum(hidden.astype(jnp.float32) * backprop, axis=1, keepdims=True)
        groups = step // CHUNK
        spread = jnp.where(lane == sub, dots, 0.0).reshape(groups, CHUNK, LANES)
        spread = jnp.sum(spread, axis=1)
        dot_ref[r * groups : (r + 1) * groups, :] = spread
        dot_ref[(r + 4) * groups : (r + 5) * groups, :] = pltpu.roll(spread, LANES - SLOTS, 1)
    parts = grad_ref.shape[0]
    wide = width // parts
    for c in range(parts):
        at = slice(c * wide, (c + 1) * wide)
        grad_ref[c] = contract(hid_ref[...], s_ref[:, at], ((0,), (0,))).astype(jnp.bfloat16)


def expert_up(me_ref, x_ref, pre_ref, own_ref, next_ref, last_ref, far_ref):
    wide = own_ref.shape[0]
    parts = x_ref.shape[1] // wide
    for shift, out in ((2, far_ref), (1, next_ref), (3, last_ref), (0, own_ref)):
        part = lax.rem(me_ref[0] + shift, parts)
        at = pl.ds(pl.multiple_of(part * wide, LANES), wide)
        out[...] = contract(x_ref[:, at], pre_ref[...], ((0,), (0,))).astype(jnp.bfloat16)


def gate_back(back_ref, code_ref, ids_ref, gates_ref, out_ref):
    experts, count = code_ref.shape
    code = code_ref[...]
    value = jnp.zeros((experts, count), jnp.float32)
    for j in range(SLOTS):
        value = jnp.where(code == float(j), back_ref[:, j : j + 1], value)
    row = lax.broadcasted_iota(jnp.int32, (experts, count), 0)
    for k in range(ids_ref.shape[0]):
        hit = row == ids_ref[k : k + 1, :]
        total = jnp.sum(jnp.where(hit, value, 0.0), axis=0, keepdims=True)
        out_ref[k : k + 1, :] = total / gates_ref[k : k + 1, :].astype(jnp.float32)


VMEM = pl.BlockSpec(memory_space=pltpu.VMEM)
SMEM = pl.BlockSpec(memory_space=pltpu.SMEM)
ANY = pl.BlockSpec(memory_space=pl.ANY)


def shards(tokens, cotangent, gate_values, expert_ids, hot_plan, expert_caps, w_up, w_down):
    experts = lax.axis_size("expert")
    groups = lax.axis_size("dp")
    count, width = tokens.shape
    top = gate_values.shape[1]
    hidden_width = w_up.shape[2]
    total = experts * CHUNK
    half = total // 2
    ids_t = expert_ids.T
    gates_t = gate_values.T
    odd = (lax.axis_index("expert") % 2).astype(jnp.int32).reshape(1)
    me = lax.axis_index("dp").astype(jnp.int32).reshape(1)
    whole = pltpu.CompilerParams(vmem_limit_bytes=56 << 20)
    part = pltpu.CompilerParams(vmem_limit_bytes=28 << 20)
    sent, code = pl.pallas_call(
        route_pack,
        out_shape=(
            jax.ShapeDtypeStruct((total, width), jnp.bfloat16),
            jax.ShapeDtypeStruct((experts, count), jnp.float32),
        ),
        in_specs=[SMEM] + [ANY] * 6,
        out_specs=(ANY, VMEM),
        scratch_shapes=[
            pltpu.VMEM((top, count), jnp.int32),
            pltpu.VMEM((top, count), jnp.bfloat16),
            pltpu.VMEM((1, experts), jnp.int32),
            pltpu.VMEM((1, experts), jnp.int32),
            pltpu.VMEM((count, width), jnp.bfloat16),
            pltpu.VMEM((count, width), jnp.bfloat16),
            pltpu.VMEM((total, width), jnp.bfloat16),
            pltpu.SemaphoreType.DMA((6 + width // 512,)),
        ],
        compiler_params=whole,
    )(odd, ids_t, gates_t, hot_plan.reshape(1, -1), expert_caps.reshape(1, -1), tokens, cotangent)
    recv = lax.all_to_all(
        sent.reshape(experts, CHUNK, width), "expert", split_axis=0, concat_axis=0, tiled=True
    )
    grad_down, dots, rows_x, grad_pre = pl.pallas_call(
        expert_down,
        out_shape=(
            jax.ShapeDtypeStruct((groups, hidden_width, width // groups), jnp.bfloat16),
            jax.ShapeDtypeStruct((experts, LANES), jnp.float32),
            jax.ShapeDtypeStruct((half, width), jnp.bfloat16),
            jax.ShapeDtypeStruct((half, hidden_width), jnp.bfloat16),
        ),
        in_specs=[VMEM] * 3,
        out_specs=(VMEM,) * 4,
        scratch_shapes=[
            pltpu.VMEM((half, width), jnp.bfloat16),
            pltpu.VMEM((half, hidden_width), jnp.bfloat16),
        ],
        compiler_params=part,
    )(recv.reshape(total, width), w_up[0], w_down[0])
    summed_down = lax.psum_scatter(
        grad_down.reshape(groups * hidden_width, -1), "dp", scatter_dimension=0, tiled=True
    )
    piece = jax.ShapeDtypeStruct((width // groups, hidden_width), jnp.bfloat16)
    own, ahead, behind, far = pl.pallas_call(
        expert_up,
        out_shape=(piece,) * 4,
        in_specs=[SMEM, VMEM, VMEM],
        out_specs=(VMEM,) * 4,
        compiler_params=part,
    )(me, rows_x, grad_pre)

    def shift(block, distance):
        return lax.ppermute(block, "dp", [(i, (i + distance) % groups) for i in range(groups)])

    far, ahead, behind = shift(far, 2), shift(ahead, 1), shift(behind, 3)
    summed_up = own.astype(jnp.float32) + far.astype(jnp.float32)
    summed_up = summed_up + ahead.astype(jnp.float32) + behind.astype(jnp.float32)
    back = lax.all_to_all(
        dots.reshape(experts, 1, LANES), "expert", split_axis=0, concat_axis=0, tiled=True
    )
    gate_grad = pl.pallas_call(
        gate_back,
        out_shape=jax.ShapeDtypeStruct((top, count), jnp.float32),
        in_specs=[VMEM] * 4,
        out_specs=VMEM,
    )(back.reshape(experts, LANES), code, ids_t, gates_t)
    return summed_up.astype(jnp.bfloat16)[None], summed_down[None], gate_grad.T


def solution(mesh):
    rows = P(("dp", "expert"), None)
    return jax.shard_map(
        shards,
        mesh=mesh,
        in_specs=(rows, rows, rows, rows, P(), P(), P("expert", None, None), P("expert", None, None)),
        out_specs=(P("expert", "dp", None), P("expert", None, "dp"), rows),
        check_vma=False,
    )
```

time: 307 us -> 274 us (0.89)
  waiting for transfers between devices: 35.5 us -> 0.03 us
  starting transfers between devices: 0.08 us -> 11.2 us
  local copies, waits for them, and re-layouts: 6.53 us -> 1.15 us
  Pallas kernels: 18 us -> 13.1 us
    reduce_scatter x2 -> x1, waiting for transfers between devices: 34.8 us -> 0.01 us  [shards(): lax.psum_scatter(grad_down.reshape(groups * hidden_width, -1), 'dp', scat...]
    ppermute x0 -> x3, starting transfers between devices: none -> 11.1 us  [shift(): lax.ppermute(block, 'dp', [(i, (i + distance) % groups) for i in range(gr...]
    unnamed x19 -> x6, local copies, waits for them, and re-layouts: 6.53 us -> 1.15 us
    pallas_call x3 -> x4, Pallas kernels: 18 us -> 13.1 us  [the longest x1 6 us: shards(): pl.pallas_call(route_pack, out_shape=(jax.ShapeDtypeStruct((total, width)...]
  transfers between devices with their start and end apart: 2 -> 4, of which waited for: 1 -> 0; matrix products, arithmetic and copies ran while one was open for 0% -> 0% of each run, Pallas kernels for 1% -> 1%
where the time goes in v2:
time: 274 us
  blocking collectives  233 us (85%)
  between operations  14.1 us (5%)
  Pallas kernels  13.1 us (5%)
  starting transfers between devices  11.2 us (4%)
    all_to_all x1, blocking collectives, shards(): lax.all_to_all(sent.reshape(experts, CHUNK, width), 'expert', split_axis=...  205 us
    all_to_all x1, blocking collectives, shards(): lax.all_to_all(dots.reshape(experts, 1, LANES), 'expert', split_axis=0, c...  28.6 us
    ppermute x3, starting transfers between devices, shift(): lax.ppermute(block, 'dp', [(i, (i + distance) % groups) for i in range(gr...  11.1 us
    pallas_call x1, Pallas kernels, shards(): pl.pallas_call(route_pack, out_shape=(jax.ShapeDtypeStruct((total, width)...  6 us
  transfers between devices with their start and end apart: 4, of which 0 were waited for; matrix products, arithmetic and copies ran while one was open for 0% of the time, Pallas kernels for 1%

profile of v2, /device:TPU:1, one launch (start us, length us, event | category | flops | bytes accessed | tf_op | source)
XLA Modules:
  0.0 273.8 jit_solution(3939094672981886082)
XLA Ops:
  7.2 0.0 reduce-scatter.2.cloned.1.call-start
  7.2 6.0 %shard_map.103 = (bf16[1024,2048]{1,0:T(8,128)(2,1)}, f32[128,128]{1,0:T(8,128)}) custom-call(s32[1]{0:T(128)} %bitcast.1.odd_ref, s32[4,128]{1,0:T(4,128)} %bitcast.26, bf16[4,128]{1,0:T(4,128)(2,1)} %bitcast.28, s32[1,128]{1,0:T(1,128)} %bitcast.31, s32[1,128]{1,0:T(1,128)} %bitcast.32, bf16[128,2048]{1,0:T(8,128)(2,1)} %x_hbm.1, bf16[128,2048]{1,0:T(8,128)(2,1)} %dy_hbm.1), custom_call_target="tpu_custom_call" | custom-call | tf_op jit(solution)/shard_map/pallas_call | solution.py:170
  13.2 0.0 copy-start
  13.2 0.0 copy-start.1
  13.3 204.7 %all_to_all.10 = bf16[128,8,2048]{2,1,0:T(8,128)(2,1)S(1)} all-to-all(bf16[128,8,2048]{2,1,0:T(8,128)(2,1)} %bitcast.24), channel_id=1, replica_groups=mesh['dp'=4,'expert'=128] {'expert'}, dimensions={0} | all-to-all | bytes 8388608 | tf_op jit(solution)/shard_map/all_to_all | solution.py:190
  218.0 0.0 copy-done
  218.0 0.0 copy-done.1
  218.0 3.9 %shard_map.104 = (bf16[4,384,512]{2,1,0:T(8,128)(2,1)S(1)}, f32[128,128]{1,0:T(8,128)S(1)}, bf16[512,2048]{1,0:T(8,128)(2,1)S(1)}, bf16[512,384]{1,0:T(8,128)(2,1)S(1)}) custom-call(bf16[1024,2048]{1,0:T(8,128)(2,1)S(1)} %bitcast.19, bf16[2048,384]{1,0:T(8,128)(2,1)S(1)} %bitcast.20, bf16[384,2048]{1,0:T(8,128)(2,1)S(1)} %bitcast.21), custom_call_target="tpu_custom_call" | custom-call | tf_op jit(solution)/shard_map/pallas_call | solution.py:193
  221.8 0.0 copy-start.2
  221.8 1.1 copy-done.2
  223.0 0.0 reduce-scatter.2.cloned.1.call-update
  223.0 1.6 shard_map.105
  224.6 4.6 %collective-permute-start = (bf16[512,384]{1,0:T(8,128)(2,1)}, bf16[512,384]{1,0:T(8,128)(2,1)S(1)}, u32[]{:S(2)}, u32[]{:S(2)}) collective-permute-start(bf16[512,384]{1,0:T(8,128)(2,1)} %get-tuple-element.17), channel_id=1, source_target_pairs={{0,256},{128,384},{256,0},{384,128},{1,257},{129,385},{257,1},{385... | collective-permute-start | bytes 1179656 | tf_op jit(solution)/shard_map/ppermute | solution.py:222
  229.3 2.2 collective-permute-start.1
  231.5 4.3 %collective-permute-start.2 = (bf16[512,384]{1,0:T(8,128)(2,1)S(1)}, bf16[512,384]{1,0:T(8,128)(2,1)S(1)}, u32[]{:S(2)}, u32[]{:S(2)}) collective-permute-start(bf16[512,384]{1,0:T(8,128)(2,1)S(1)} %get-tuple-element.19), channel_id=1, source_target_pairs={{0,384},{128,0},{256,128},{384,256},{1,385},{129,1},{257,129},{385... | collective-permute-start | bytes 1179656 | tf_op jit(solution)/shard_map/ppermute | solution.py:222
  235.8 28.6 %all_to_all.11 = f32[128,1,128]{2,1,0:T(1,128)} all-to-all(f32[128,1,128]{2,1,0:T(1,128)S(1)} %bitcast.23), channel_id=1, replica_groups=mesh['dp'=4,'expert'=128] {'expert'}, dimensions={0} | all-to-all | bytes 131072 | tf_op jit(solution)/shard_map/all_to_all | solution.py:227
  264.4 1.6 shard_map.106
  266.0 0.0 collective-permute-done
  266.0 0.0 collective-permute-done.1
  266.0 0.0 collective-permute-done.2
  266.0 0.9 fusion
  266.9 0.0 reduce-scatter.2.cloned.1.call-done
Async XLA Ops:
  7.2 259.8 %reduce-scatter.2.cloned.1.call-start = ((), (), s32[]{:S(2)}) async-start(), calls=%async_computation.3 | async-start | bytes 1966080 | tf_op jit(solution)/shard_map/reduce_scatter | solution.py:209
  13.2 204.7 %copy-start = (bf16[1,2048,384]{2,1,0:T(8,128)(2,1)S(1)}, bf16[1,2048,384]{2,1,0:T(8,128)(2,1)}, u32[]{:S(2)}) copy-start(bf16[1,2048,384]{2,1,0:T(8,128)(2,1)} %param.14) | copy-start | bytes 4718596
  13.2 204.7 %copy-start.1 = (bf16[1,384,2048]{2,1,0:T(8,128)(2,1)S(1)}, bf16[1,384,2048]{2,1,0:T(8,128)(2,1)}, u32[]{:S(2)}) copy-start(bf16[1,384,2048]{2,1,0:T(8,128)(2,1)} %param.15) | copy-start | bytes 4718596
  221.8 1.1 copy-start.2
  224.6 41.4 %collective-permute-start = (bf16[512,384]{1,0:T(8,128)(2,1)}, bf16[512,384]{1,0:T(8,128)(2,1)S(1)}, u32[]{:S(2)}, u32[]{:S(2)}) collective-permute-start(bf16[512,384]{1,0:T(8,128)(2,1)} %get-tuple-element.17), channel_id=1, source_target_pairs={{0,256},{128,384},{256,0},{384,128},{1,257},{129,385},{257,1},{385... | collective-permute-start | bytes 1179656 | tf_op jit(solution)/shard_map/ppermute | solution.py:222
  229.3 36.7 %collective-permute-start.1 = (bf16[512,384]{1,0:T(8,128)(2,1)}, bf16[512,384]{1,0:T(8,128)(2,1)S(1)}, u32[]{:S(2)}, u32[]{:S(2)}) collective-permute-start(bf16[512,384]{1,0:T(8,128)(2,1)} %get-tuple-element.18), channel_id=1, source_target_pairs={{0,128},{128,256},{256,384},{384,0},{1,129},{129,257},{257,385},{3... | collective-permute-start | bytes 1179656 | tf_op jit(solution)/shard_map/ppermute | solution.py:222
  231.5 34.5 %collective-permute-start.2 = (bf16[512,384]{1,0:T(8,128)(2,1)S(1)}, bf16[512,384]{1,0:T(8,128)(2,1)S(1)}, u32[]{:S(2)}, u32[]{:S(2)}) collective-permute-start(bf16[512,384]{1,0:T(8,128)(2,1)S(1)} %get-tuple-element.19), channel_id=1, source_target_pairs={{0,384},{128,0},{256,128},{384,256},{1,385},{129,1},{257,129},{385... | collective-permute-start | bytes 1179656 | tf_op jit(solution)/shard_map/ppermute | solution.py:222
Sparse Core Ops, SparseCore 0:
  223.1 38.6 reduce-scatter.1

commit v3 on v2

--- a/solution.py
+++ b/solution.py
@@ -91,16 +91,38 @@
         copy.wait()
 
 
-def expert_down(
-    recv_ref, up_ref, down_ref, grad_ref, dot_ref, x_ref, pre_ref, s_ref, hid_ref
+def write_piece(part, x_ref, s_ref, hid_ref, pre_ref, out_ref):
+    parts = x_ref.shape[1] * pre_ref.shape[1] * 2 // (out_ref.shape[0] * LANES)
+    wide = x_ref.shape[1] // parts
+    tall = pre_ref.shape[1]
+    at = pl.ds(pl.multiple_of(part * wide, LANES), wide)
+    up = contract(x_ref[:, at], pre_ref[...], ((0,), (0,))).astype(jnp.bfloat16)
+    for c in range(tall // LANES):
+        out_ref[c * wide : (c + 1) * wide, :] = up[:, c * LANES : (c + 1) * LANES]
+    down = contract(hid_ref[...], s_ref[:, at], ((0,), (0,))).astype(jnp.bfloat16)
+    base = wide * tall // LANES
+    for c in range(wide // LANES):
+        out_ref[base + c * tall : base + (c + 1) * tall, :] = down[:, c * LANES : (c + 1) * LANES]
+
+
+def expert_rows(
+    me_ref, recv_hbm, up_ref, down_ref, own_ref, ahead_ref, behind_ref, far_ref, dot_ref,
+    recv_ref, x_ref, s_ref, hid_ref, pre_ref, sems,
 ):
     half, width = x_ref.shape
     step = half // 4
+    copies = []
+    for n in range(8):
+        at = pl.ds((n // 2) * step + (n % 2) * half, step)
+        copies.append(pltpu.make_async_copy(recv_hbm.at[at, :], recv_ref.at[at, :], sems.at[n]))
+        copies[-1].start()
     lower = lax.broadcasted_iota(jnp.int32, (step, width), 0) % CHUNK < SLOTS
     lane = lax.broadcasted_iota(jnp.int32, (step, LANES), 1)
     sub = lax.broadcasted_iota(jnp.int32, (step, LANES), 0) % CHUNK
     for r in range(4):
         at = slice(r * step, (r + 1) * step)
+        copies[2 * r].wait()
+        copies[2 * r + 1].wait()
         first = recv_ref[at, :]
         second = recv_ref[r * step + half : (r + 1) * step + half, :]
         x = jnp.where(lower, first, pltpu.roll(second, SLOTS, 0))
@@ -119,20 +141,24 @@
         spread = jnp.sum(spread, axis=1)
         dot_ref[r * groups : (r + 1) * groups, :] = spread
         dot_ref[(r + 4) * groups : (r + 5) * groups, :] = pltpu.roll(spread, LANES - SLOTS, 1)
-    parts = grad_ref.shape[0]
-    wide = width // parts
-    for c in range(parts):
-        at = slice(c * wide, (c + 1) * wide)
-        grad_ref[c] = contract(hid_ref[...], s_ref[:, at], ((0,), (0,))).astype(jnp.bfloat16)
-
-
-def expert_up(me_ref, x_ref, pre_ref, own_ref, next_ref, last_ref, far_ref):
-    wide = own_ref.shape[0]
-    parts = x_ref.shape[1] // wide
-    for shift, out in ((2, far_ref), (1, next_ref), (3, last_ref), (0, own_ref)):
-        part = lax.rem(me_ref[0] + shift, parts)
-        at = pl.ds(pl.multiple_of(part * wide, LANES), wide)
-        out[...] = contract(x_ref[:, at], pre_ref[...], ((0,), (0,))).astype(jnp.bfloat16)
+    parts = width * pre_ref.shape[1] * 2 // (own_ref.shape[0] * LANES)
+    for shift, out_ref in ((2, far_ref), (1, ahead_ref), (3, behind_ref), (0, own_ref)):
+        write_piece(lax.rem(me_ref[0] + shift, parts), x_ref, s_ref, hid_ref, pre_ref, out_ref)
+
+
+def add_pieces(own_ref, far_ref, ahead_ref, behind_ref, up_ref, down_ref):
+    refs = (own_ref, far_ref, ahead_ref, behind_ref)
+    wide, tall = up_ref.shape
+    base = wide * tall // LANES
+
+    def total(at):
+        first, second, third, fourth = [ref[at, :].astype(jnp.float32) for ref in refs]
+        return ((first + second) + (third + fourth)).astype(jnp.bfloat16)
+
+    for c in range(tall // LANES):
+        up_ref[:, c * LANES : (c + 1) * LANES] = total(slice(c * wide, (c + 1) * wide))
+    for c in range(wide // LANES):
+        down_ref[:, c * LANES : (c + 1) * LANES] = total(slice(base + c * tall, base + (c + 1) * tall))
 
 
 def gate_back(back_ref, code_ref, ids_ref, gates_ref, out_ref):
@@ -166,7 +192,7 @@
     odd = (lax.axis_index("expert") % 2).astype(jnp.int32).reshape(1)
     me = lax.axis_index("dp").astype(jnp.int32).reshape(1)
     whole = pltpu.CompilerParams(vmem_limit_bytes=56 << 20)
-    part = pltpu.CompilerParams(vmem_limit_bytes=28 << 20)
+    part = pltpu.CompilerParams(vmem_limit_bytes=24 << 20)
     sent, code = pl.pallas_call(
         route_pack,
         out_shape=(
@@ -190,50 +216,49 @@
     recv = lax.all_to_all(
         sent.reshape(experts, CHUNK, width), "expert", split_axis=0, concat_axis=0, tiled=True
     )
-    grad_down, dots, rows_x, grad_pre = pl.pallas_call(
-        expert_down,
-        out_shape=(
-            jax.ShapeDtypeStruct((groups, hidden_width, width // groups), jnp.bfloat16),
-            jax.ShapeDtypeStruct((experts, LANES), jnp.float32),
-            jax.ShapeDtypeStruct((half, width), jnp.bfloat16),
-            jax.ShapeDtypeStruct((half, hidden_width), jnp.bfloat16),
-        ),
-        in_specs=[VMEM] * 3,
-        out_specs=(VMEM,) * 4,
+    wide = width // groups
+    piece = jax.ShapeDtypeStruct((2 * wide * hidden_width // LANES, LANES), jnp.bfloat16)
+    own, ahead, behind, far, dots = pl.pallas_call(
+        expert_rows,
+        out_shape=(piece,) * 4 + (jax.ShapeDtypeStruct((experts, LANES), jnp.float32),),
+        in_specs=[SMEM, ANY, VMEM, VMEM],
+        out_specs=(VMEM,) * 5,
         scratch_shapes=[
+            pltpu.VMEM((total, width), jnp.bfloat16),
+            pltpu.VMEM((half, width), jnp.bfloat16),
             pltpu.VMEM((half, width), jnp.bfloat16),
             pltpu.VMEM((half, hidden_width), jnp.bfloat16),
+            pltpu.VMEM((half, hidden_width), jnp.bfloat16),
+            pltpu.SemaphoreType.DMA((8,)),
         ],
         compiler_params=part,
-    )(recv.reshape(total, width), w_up[0], w_down[0])
-    summed_down = lax.psum_scatter(
-        grad_down.reshape(groups * hidden_width, -1), "dp", scatter_dimension=0, tiled=True
-    )
-    piece = jax.ShapeDtypeStruct((width // groups, hidden_width), jnp.bfloat16)
-    own, ahead, behind, far = pl.pallas_call(
-        expert_up,
-        out_shape=(piece,) * 4,
-        in_specs=[SMEM, VMEM, VMEM],
-        out_specs=(VMEM,) * 4,
-        compiler_params=part,
-    )(me, rows_x, grad_pre)
+    )(me, recv.reshape(total, width), w_up[0], w_down[0])
 
     def shift(block, distance):
         return lax.ppermute(block, "dp", [(i, (i + distance) % groups) for i in range(groups)])
 
     far, ahead, behind = shift(far, 2), shift(ahead, 1), shift(behind, 3)
-    summed_up = own.astype(jnp.float32) + far.astype(jnp.float32)
-    summed_up = summed_up + ahead.astype(jnp.float32) + behind.astype(jnp.float32)
+    summed_up, summed_down = pl.pallas_call(
+        add_pieces,
+        out_shape=(
+            jax.ShapeDtypeStruct((wide, hidden_width), jnp.bfloat16),
+            jax.ShapeDtypeStruct((hidden_width, wide), jnp.bfloat16),
+        ),
+        in_specs=[VMEM] * 4,
+        out_specs=(VMEM,) * 2,
+        compiler_params=pltpu.CompilerParams(vmem_limit_bytes=12 << 20),
+    )(own, far, ahead, behind)
     back = lax.all_to_all(
         dots.reshape(experts, 1, LANES), "expert", split_axis=0, concat_axis=0, tiled=True
     )
     gate_grad = pl.pallas_call(
         gate_back,
         out_shape=jax.ShapeDtypeStruct((top, count), jnp.float32),
+        compiler_params=pltpu.CompilerParams(vmem_limit_bytes=8 << 20),
         in_specs=[VMEM] * 4,
         out_specs=VMEM,
     )(back.reshape(experts, LANES), code, ids_t, gates_t)
-    return summed_up.astype(jnp.bfloat16)[None], summed_down[None], gate_grad.T
+    return summed_up[None], summed_down[None], gate_grad.T
 
 
 def solution(mesh):

time: 274 us -> 263 us (0.960)
  blocking collectives: 233 us -> 28.7 us
  waiting for transfers between devices: 0.03 us -> 183 us
  starting transfers between devices: 11.2 us -> 32.4 us
  between operations: 14.1 us -> 0.74 us
    all_to_all x1 -> x0, blocking collectives: 205 us -> none  [shards(): lax.all_to_all(sent.reshape(experts, CHUNK, width), 'expert', split_axis=...]
    all_to_all x0 -> x1, waiting for transfers between devices: none -> 183 us  [shards(): lax.all_to_all(sent.reshape(experts, CHUNK, width), 'expert', split_axis=...]
    all_to_all x0 -> x1, starting transfers between devices: none -> 21.3 us  [shards(): lax.all_to_all(sent.reshape(experts, CHUNK, width), 'expert', split_axis=...]
    pallas_call x2, Pallas kernels: 5.47 us -> 8.99 us  [the longest x1 7.83 us: shards(): pl.pallas_call(expert_rows, out_shape=(piece,) * 4 + (jax.ShapeDtypeStruc...]
  transfers between devices with their start and end apart: 4 -> 4, of which waited for: 0 -> 1; matrix products, arithmetic and copies ran while one was open for 0% -> 0% of each run, Pallas kernels for 1% -> 0%
where the time goes in v3:
time: 263 us; the launch traced here: 261 us
  waiting for transfers between devices  183 us (70%)
  starting transfers between devices  32.4 us (12%)
  blocking collectives  28.7 us (11%)
  Pallas kernels  15.7 us (6%)
    all_to_all x1, waiting for transfers between devices, shards(): lax.all_to_all(sent.reshape(experts, CHUNK, width), 'expert', split_axis=...  183 us
    all_to_all x1, blocking collectives, shards(): lax.all_to_all(dots.reshape(experts, 1, LANES), 'expert', split_axis=0, c...  28.7 us
    all_to_all x1, starting transfers between devices, shards(): lax.all_to_all(sent.reshape(experts, CHUNK, width), 'expert', split_axis=...  21.3 us
    ppermute x3, starting transfers between devices, shift(): lax.ppermute(block, 'dp', [(i, (i + distance) % groups) for i in range(gr...  11.1 us
    pallas_call x1, Pallas kernels, shards(): pl.pallas_call(expert_rows, out_shape=(piece,) * 4 + (jax.ShapeDtypeStruc...  7.83 us
    pallas_call x1, Pallas kernels, shards(): pl.pallas_call(route_pack, out_shape=(jax.ShapeDtypeStruct((total, width)...  5.99 us
  transfers between devices with their start and end apart: 4, of which 1 were waited for; matrix products, arithmetic and copies ran while one was open for 0% of the time, Pallas kernels for 0%

profile of v3, /device:TPU:1, one launch (start us, length us, event | category | flops | bytes accessed | tf_op | source)
XLA Modules:
  0.0 261.1 jit_solution(16454913815079585270)
XLA Ops:
  0.6 6.0 %shard_map.103 = (bf16[1024,2048]{1,0:T(8,128)(2,1)}, f32[128,128]{1,0:T(8,128)}) custom-call(s32[1]{0:T(128)} %bitcast.1.odd_ref, s32[4,128]{1,0:T(4,128)} %bitcast.21, bf16[4,128]{1,0:T(4,128)(2,1)} %bitcast.23, s32[1,128]{1,0:T(1,128)} %bitcast.27, s32[1,128]{1,0:T(1,128)} %bitcast.28, bf16[128,2048]{1,0:T(8,128)(2,1)} %x_hbm.1, bf16[128,2048]{1,0:T(8,128)(2,1)} %dy_hbm.1), custom_call_target="tpu_custom_call" | custom-call | tf_op jit(solution)/shard_map/pallas_call | solution.py:196
  6.6 0.0 copy-start
  6.7 0.0 copy-start.1
  6.7 21.3 %all-to-all-start = ((bf16[128,8,2048]{2,1,0:T(8,128)(2,1)}), bf16[128,8,2048]{2,1,0:T(8,128)(2,1)}, u32[]{:S(2)}, u32[]{:S(2)}) async-start(bf16[128,8,2048]{2,1,0:T(8,128)(2,1)} %bitcast.25), calls=%async_computation | async-start | bytes 8388608 | tf_op jit(solution)/shard_map/all_to_all | solution.py:216
  28.0 0.0 copy-start.2
  28.0 0.0 copy-start.3
  28.0 0.0 copy-start.4
  28.0 183.5 %all-to-all-done = bf16[128,8,2048]{2,1,0:T(8,128)(2,1)} async-done(((bf16[128,8,2048]{2,1,0:T(8,128)(2,1)}), bf16[128,8,2048]{2,1,0:T(8,128)(2,1)}, u32[]{:S(2)}, u32[]{:S(2)}) %all-to-all-start) | async-done | bytes 4194336 | tf_op jit(solution)/shard_map/all_to_all | solution.py:216
  211.5 0.0 copy-done
  211.5 0.0 copy-done.1
  211.5 7.8 %shard_map.104 = (bf16[3072,128]{1,0:T(8,128)(2,1)S(1)}, bf16[3072,128]{1,0:T(8,128)(2,1)S(1)}, bf16[3072,128]{1,0:T(8,128)(2,1)S(1)}, bf16[3072,128]{1,0:T(8,128)(2,1)S(1)}, f32[128,128]{1,0:T(8,128)S(1)}) custom-call(s32[1]{0:T(128)} %bitcast.me_ref, bf16[1024,2048]{1,0:T(8,128)(2,1)} %bitcast.7.recv_hbm, bf16[2048,384]{1,0:T(8,128)(2,1)S(1)} %bitcast.17, ...), custom_call_target="tpu_custom_call" | custom-call | tf_op jit(solution)/shard_map/pallas_call | solution.py:221
  219.3 4.7 %collective-permute-start = (bf16[3072,128]{1,0:T(8,128)(2,1)S(1)}, bf16[3072,128]{1,0:T(8,128)(2,1)S(1)}, u32[]{:S(2)}, u32[]{:S(2)}) collective-permute-start(bf16[3072,128]{1,0:T(8,128)(2,1)S(1)} %get-tuple-element.14), channel_id=1, source_target_pairs={{0,256},{128,384},{256,0},{384,128},{1,257},{129,385},{257,1},{385... | collective-permute-start | bytes 2359304 | tf_op jit(solution)/shard_map/ppermute | solution.py:238
  224.0 2.2 collective-permute-start.1
  226.2 4.3 %collective-permute-start.2 = (bf16[3072,128]{1,0:T(8,128)(2,1)S(1)}, bf16[3072,128]{1,0:T(8,128)(2,1)S(1)}, u32[]{:S(2)}, u32[]{:S(2)}) collective-permute-start(bf16[3072,128]{1,0:T(8,128)(2,1)S(1)} %get-tuple-element.16), channel_id=1, source_target_pairs={{0,384},{128,0},{256,128},{384,256},{1,385},{129,1},{257,129},{385... | collective-permute-start | bytes 2359304 | tf_op jit(solution)/shard_map/ppermute | solution.py:238
  230.5 28.7 %all_to_all.10 = f32[128,1,128]{2,1,0:T(1,128)S(1)} all-to-all(f32[128,1,128]{2,1,0:T(1,128)S(1)} %bitcast.20), channel_id=1, replica_groups=mesh['dp'=4,'expert'=128] {'expert'}, dimensions={0} | all-to-all | bytes 131072 | tf_op jit(solution)/shard_map/all_to_all | solution.py:251
  259.2 0.0 copy-done.2
  259.2 0.0 copy-done.3
  259.2 0.0 copy-done.4
  259.2 0.7 shard_map.106
  259.9 0.0 collective-permute-done.far_ref
  259.9 0.0 collective-permute-done.1.ahead_ref
  259.9 0.0 collective-permute-done.2.behind_ref
  259.9 1.2 shard_map.105
Async XLA Ops:
  6.6 204.8 %copy-start = (bf16[1,2048,384]{2,1,0:T(8,128)(2,1)S(1)}, bf16[1,2048,384]{2,1,0:T(8,128)(2,1)}, u32[]{:S(2)}) copy-start(bf16[1,2048,384]{2,1,0:T(8,128)(2,1)} %param.14) | copy-start | bytes 4718596
  6.7 204.8 %copy-start.1 = (bf16[1,384,2048]{2,1,0:T(8,128)(2,1)S(1)}, bf16[1,384,2048]{2,1,0:T(8,128)(2,1)}, u32[]{:S(2)}) copy-start(bf16[1,384,2048]{2,1,0:T(8,128)(2,1)} %param.15) | copy-start | bytes 4718596
  6.7 204.8 %all-to-all-start = ((bf16[128,8,2048]{2,1,0:T(8,128)(2,1)}), bf16[128,8,2048]{2,1,0:T(8,128)(2,1)}, u32[]{:S(2)}, u32[]{:S(2)}) async-start(bf16[128,8,2048]{2,1,0:T(8,128)(2,1)} %bitcast.25), calls=%async_computation | async-start | bytes 8388608 | tf_op jit(solution)/shard_map/all_to_all | solution.py:216
  28.0 231.2 %copy-start.2 = (f32[128,128]{1,0:T(8,128)S(1)}, f32[128,128]{1,0:T(8,128)}, u32[]{:S(2)}) copy-start(f32[128,128]{1,0:T(8,128)} %get-tuple-element.20.code_ref) | copy-start | bytes 196612
  28.0 231.2 %copy-start.3 = (s32[128,4]{0,1:T(4,128)S(1)}, s32[128,4]{0,1:T(4,128)}, u32[]{:S(2)}) copy-start(s32[128,4]{0,1:T(4,128)} %param.11) | copy-start | bytes 6148
  28.0 231.2 %copy-start.4 = (bf16[128,4]{0,1:T(4,128)(2,1)S(1)}, bf16[128,4]{0,1:T(4,128)(2,1)}, u32[]{:S(2)}) copy-start(bf16[128,4]{0,1:T(4,128)(2,1)} %param.10) | copy-start | bytes 3076
  219.3 40.6 %collective-permute-start = (bf16[3072,128]{1,0:T(8,128)(2,1)S(1)}, bf16[3072,128]{1,0:T(8,128)(2,1)S(1)}, u32[]{:S(2)}, u32[]{:S(2)}) collective-permute-start(bf16[3072,128]{1,0:T(8,128)(2,1)S(1)} %get-tuple-element.14), channel_id=1, source_target_pairs={{0,256},{128,384},{256,0},{384,128},{1,257},{129,385},{257,1},{385... | collective-permute-start | bytes 2359304 | tf_op jit(solution)/shard_map/ppermute | solution.py:238
  224.0 35.9 %collective-permute-start.1 = (bf16[3072,128]{1,0:T(8,128)(2,1)S(1)}, bf16[3072,128]{1,0:T(8,128)(2,1)S(1)}, u32[]{:S(2)}, u32[]{:S(2)}) collective-permute-start(bf16[3072,128]{1,0:T(8,128)(2,1)S(1)} %get-tuple-element.15), channel_id=1, source_target_pairs={{0,128},{128,256},{256,384},{384,0},{1,129},{129,257},{257,385},{3... | collective-permute-start | bytes 2359304 | tf_op jit(solution)/shard_map/ppermute | solution.py:238
  226.2 33.7 %collective-permute-start.2 = (bf16[3072,128]{1,0:T(8,128)(2,1)S(1)}, bf16[3072,128]{1,0:T(8,128)(2,1)S(1)}, u32[]{:S(2)}, u32[]{:S(2)}) collective-permute-start(bf16[3072,128]{1,0:T(8,128)(2,1)S(1)} %get-tuple-element.16), channel_id=1, source_target_pairs={{0,384},{128,0},{256,128},{384,256},{1,385},{129,1},{257,129},{385... | collective-permute-start | bytes 2359304 | tf_op jit(solution)/shard_map/ppermute | solution.py:238

commit v4 on v3

--- a/solution.py
+++ b/solution.py
@@ -15,7 +15,7 @@
 
 
 def route_pack(
-    odd_ref, ids_hbm, gates_hbm, hot_hbm, caps_hbm, x_hbm, dy_hbm, sent_hbm, code_ref,
+    place_ref, ids_hbm, gates_hbm, hot_hbm, caps_hbm, x_hbm, dy_hbm, sent_hbm, code_ref,
     ids_ref, gates_ref, hot_ref, caps_ref, x_ref, dy_ref, sent_ref, sems,
 ):
     pairs = (
@@ -56,7 +56,7 @@
         gate = jnp.where(hit, gates[:, at], gate)
     rank = contract(below, picked.astype(jnp.bfloat16), ((1,), (0,)))
     admitted = jnp.where(rank < caps_ref[...].astype(jnp.float32), picked, 0.0)
-    moves = hot_ref[...].astype(jnp.float32) * odd_ref[0].astype(jnp.float32)
+    moves = hot_ref[...].astype(jnp.float32) * place_ref[1].astype(jnp.float32)
     moved = admitted * moves
     stay = admitted - moved
     moved_next = pltpu.roll(moved, 1, 1)
@@ -99,30 +99,23 @@
     up = contract(x_ref[:, at], pre_ref[...], ((0,), (0,))).astype(jnp.bfloat16)
     for c in range(tall // LANES):
         out_ref[c * wide : (c + 1) * wide, :] = up[:, c * LANES : (c + 1) * LANES]
-    down = contract(hid_ref[...], s_ref[:, at], ((0,), (0,))).astype(jnp.bfloat16)
+    down = contract(hid_ref[...], s_ref[:, at], ((1,), (0,))).astype(jnp.bfloat16)
     base = wide * tall // LANES
     for c in range(wide // LANES):
         out_ref[base + c * tall : base + (c + 1) * tall, :] = down[:, c * LANES : (c + 1) * LANES]
 
 
 def expert_rows(
-    me_ref, recv_hbm, up_ref, down_ref, own_ref, ahead_ref, behind_ref, far_ref, dot_ref,
-    recv_ref, x_ref, s_ref, hid_ref, pre_ref, sems,
+    place_ref, recv_ref, up_ref, down_ref, own_ref, ahead_ref, behind_ref, far_ref, dot_ref,
+    x_ref, s_ref, hid_ref, pre_ref,
 ):
     half, width = x_ref.shape
     step = half // 4
-    copies = []
-    for n in range(8):
-        at = pl.ds((n // 2) * step + (n % 2) * half, step)
-        copies.append(pltpu.make_async_copy(recv_hbm.at[at, :], recv_ref.at[at, :], sems.at[n]))
-        copies[-1].start()
     lower = lax.broadcasted_iota(jnp.int32, (step, width), 0) % CHUNK < SLOTS
     lane = lax.broadcasted_iota(jnp.int32, (step, LANES), 1)
     sub = lax.broadcasted_iota(jnp.int32, (step, LANES), 0) % CHUNK
     for r in range(4):
         at = slice(r * step, (r + 1) * step)
-        copies[2 * r].wait()
-        copies[2 * r + 1].wait()
         first = recv_ref[at, :]
         second = recv_ref[r * step + half : (r + 1) * step + half, :]
         x = jnp.where(lower, first, pltpu.roll(second, SLOTS, 0))
@@ -133,7 +126,7 @@
         backprop = contract(s, down_ref[...], ((1,), (1,)))
         sigma = jax.nn.sigmoid(preact)
         hidden = (preact * sigma).astype(jnp.bfloat16)
-        hid_ref[at, :] = hidden
+        hid_ref[:, at] = hidden.T
         pre_ref[at, :] = (backprop * sigma * (1.0 + preact * (1.0 - sigma))).astype(jnp.bfloat16)
         dots = jnp.sum(hidden.astype(jnp.float32) * backprop, axis=1, keepdims=True)
         groups = step // CHUNK
@@ -143,7 +136,7 @@
         dot_ref[(r + 4) * groups : (r + 5) * groups, :] = pltpu.roll(spread, LANES - SLOTS, 1)
     parts = width * pre_ref.shape[1] * 2 // (own_ref.shape[0] * LANES)
     for shift, out_ref in ((2, far_ref), (1, ahead_ref), (3, behind_ref), (0, own_ref)):
-        write_piece(lax.rem(me_ref[0] + shift, parts), x_ref, s_ref, hid_ref, pre_ref, out_ref)
+        write_piece(lax.rem(place_ref[0] + shift, parts), x_ref, s_ref, hid_ref, pre_ref, out_ref)
 
 
 def add_pieces(own_ref, far_ref, ahead_ref, behind_ref, up_ref, down_ref):
@@ -189,8 +182,7 @@
     half = total // 2
     ids_t = expert_ids.T
     gates_t = gate_values.T
-    odd = (lax.axis_index("expert") % 2).astype(jnp.int32).reshape(1)
-    me = lax.axis_index("dp").astype(jnp.int32).reshape(1)
+    place = jnp.stack([lax.axis_index("dp"), lax.axis_index("expert") % 2]).astype(jnp.int32)
     whole = pltpu.CompilerParams(vmem_limit_bytes=56 << 20)
     part = pltpu.CompilerParams(vmem_limit_bytes=24 << 20)
     sent, code = pl.pallas_call(
@@ -212,7 +204,7 @@
             pltpu.SemaphoreType.DMA((6 + width // 512,)),
         ],
         compiler_params=whole,
-    )(odd, ids_t, gates_t, hot_plan.reshape(1, -1), expert_caps.reshape(1, -1), tokens, cotangent)
+    )(place, ids_t, gates_t, hot_plan.reshape(1, -1), expert_caps.reshape(1, -1), tokens, cotangent)
     recv = lax.all_to_all(
         sent.reshape(experts, CHUNK, width), "expert", split_axis=0, concat_axis=0, tiled=True
     )
@@ -221,18 +213,16 @@
     own, ahead, behind, far, dots = pl.pallas_call(
         expert_rows,
         out_shape=(piece,) * 4 + (jax.ShapeDtypeStruct((experts, LANES), jnp.float32),),
-        in_specs=[SMEM, ANY, VMEM, VMEM],
+        in_specs=[SMEM] + [VMEM] * 3,
         out_specs=(VMEM,) * 5,
         scratch_shapes=[
-            pltpu.VMEM((total, width), jnp.bfloat16),
             pltpu.VMEM((half, width), jnp.bfloat16),
             pltpu.VMEM((half, width), jnp.bfloat16),
+            pltpu.VMEM((hidden_width, half), jnp.bfloat16),
             pltpu.VMEM((half, hidden_width), jnp.bfloat16),
-            pltpu.VMEM((half, hidden_width), jnp.bfloat16),
-            pltpu.SemaphoreType.DMA((8,)),
         ],
         compiler_params=part,
-    )(me, recv.reshape(total, width), w_up[0], w_down[0])
+    )(place, recv.reshape(total, width), w_up[0], w_down[0])
 
     def shift(block, distance):
         return lax.ppermute(block, "dp", [(i, (i + distance) % groups) for i in range(groups)])

time: 263 us -> 263 us (level)
  blocking collectives: 28.7 us -> 233 us
  waiting for transfers between devices: 183 us -> 0.01 us
  starting transfers between devices: 32.4 us -> 11.1 us
    all_to_all x0 -> x1, blocking collectives: none -> 205 us  [shards(): lax.all_to_all(sent.reshape(experts, CHUNK, width), 'expert', split_axis=...]
    all_to_all x1 -> x0, waiting for transfers between devices: 183 us -> none  [shards(): lax.all_to_all(sent.reshape(experts, CHUNK, width), 'expert', split_axis=...]
    all_to_all x1 -> x0, starting transfers between devices: 21.3 us -> none  [shards(): lax.all_to_all(sent.reshape(experts, CHUNK, width), 'expert', split_axis=...]
  transfers between devices with their start and end apart: 4 -> 3, of which waited for: 1 -> 0; matrix products, arithmetic and copies ran while one was open for 0% -> 0% of each run, Pallas kernels for 0% -> 0%
where the time goes in v4:
time: 263 us; the launch traced here: 261 us
  blocking collectives  233 us (89%)
  Pallas kernels  15 us (6%)
  starting transfers between devices  11.1 us (4%)
    all_to_all x1, blocking collectives, shards(): lax.all_to_all(sent.reshape(experts, CHUNK, width), 'expert', split_axis=...  205 us
    all_to_all x1, blocking collectives, shards(): lax.all_to_all(dots.reshape(experts, 1, LANES), 'expert', split_axis=0, c...  28.7 us
    ppermute x3, starting transfers between devices, shift(): lax.ppermute(block, 'dp', [(i, (i + distance) % groups) for i in range(gr...  11.1 us
    pallas_call x1, Pallas kernels, shards(): pl.pallas_call(route_pack, out_shape=(jax.ShapeDtypeStruct((total, width)...  6.67 us
    pallas_call x1, Pallas kernels, shards(): pl.pallas_call(expert_rows, out_shape=(piece,) * 4 + (jax.ShapeDtypeStruc...  6.42 us
  transfers between devices with their start and end apart: 3, of which 0 were waited for; matrix products, arithmetic and copies ran while one was open for 0% of the time, Pallas kernels for 0%

profile of v4, /device:TPU:1, one launch (start us, length us, event | category | flops | bytes accessed | tf_op | source)
XLA Modules:
  0.0 260.8 jit_solution(10216232070103590115)
XLA Ops:
  0.6 0.6 pad_add_fusion.place_ref
  1.2 6.7 %shard_map.103 = (bf16[1024,2048]{1,0:T(8,128)(2,1)}, f32[128,128]{1,0:T(8,128)}) custom-call(s32[2]{0:T(128)} %pad_add_fusion.place_ref, s32[4,128]{1,0:T(4,128)} %bitcast.22, bf16[4,128]{1,0:T(4,128)(2,1)} %bitcast.24, s32[1,128]{1,0:T(1,128)} %bitcast.28, s32[1,128]{1,0:T(1,128)} %bitcast.29, bf16[128,2048]{1,0:T(8,128)(2,1)} %x_hbm.1, ...), custom_call_target="tpu_custom_call" | custom-call | tf_op jit(solution)/shard_map/pallas_call | solution.py:188
  7.9 0.0 copy-start
  7.9 0.0 copy-start.1
  7.9 0.0 copy-start.5
  7.9 204.7 %all_to_all.10 = bf16[128,8,2048]{2,1,0:T(8,128)(2,1)S(1)} all-to-all(bf16[128,8,2048]{2,1,0:T(8,128)(2,1)} %bitcast.26), channel_id=1, replica_groups=mesh['dp'=4,'expert'=128] {'expert'}, dimensions={0} | all-to-all | bytes 8388608 | tf_op jit(solution)/shard_map/all_to_all | solution.py:208
  212.6 0.0 copy-start.2
  212.6 0.0 copy-start.3
  212.6 0.0 copy-start.4
  212.6 0.0 copy-done
  212.6 0.0 copy-done.1
  212.7 0.0 copy-done.5
  212.7 6.4 %shard_map.104 = (bf16[3072,128]{1,0:T(8,128)(2,1)S(1)}, bf16[3072,128]{1,0:T(8,128)(2,1)S(1)}, bf16[3072,128]{1,0:T(8,128)(2,1)S(1)}, bf16[3072,128]{1,0:T(8,128)(2,1)S(1)}, f32[128,128]{1,0:T(8,128)S(1)}) custom-call(s32[2]{0:T(128)S(1)} %copy-done.5, bf16[1024,2048]{1,0:T(8,128)(2,1)S(1)} %bitcast.17, bf16[2048,384]{1,0:T(8,128)(2,1)S(1)} %bitcast.18, ...), custom_call_target="tpu_custom_call" | custom-call | tf_op jit(solution)/shard_map/pallas_call | solution.py:213
  219.1 4.6 %collective-permute-start = (bf16[3072,128]{1,0:T(8,128)(2,1)S(1)}, bf16[3072,128]{1,0:T(8,128)(2,1)S(1)}, u32[]{:S(2)}, u32[]{:S(2)}) collective-permute-start(bf16[3072,128]{1,0:T(8,128)(2,1)S(1)} %get-tuple-element.14), channel_id=1, source_target_pairs={{0,256},{128,384},{256,0},{384,128},{1,257},{129,385},{257,1},{385... | collective-permute-start | bytes 2359304 | tf_op jit(solution)/shard_map/ppermute | solution.py:228
  223.7 2.2 collective-permute-start.1
  225.9 4.3 %collective-permute-start.2 = (bf16[3072,128]{1,0:T(8,128)(2,1)S(1)}, bf16[3072,128]{1,0:T(8,128)(2,1)S(1)}, u32[]{:S(2)}, u32[]{:S(2)}) collective-permute-start(bf16[3072,128]{1,0:T(8,128)(2,1)S(1)} %get-tuple-element.16), channel_id=1, source_target_pairs={{0,384},{128,0},{256,128},{384,256},{1,385},{129,1},{257,129},{385... | collective-permute-start | bytes 2359304 | tf_op jit(solution)/shard_map/ppermute | solution.py:228
  230.3 28.7 %all_to_all.11 = f32[128,1,128]{2,1,0:T(1,128)S(1)} all-to-all(f32[128,1,128]{2,1,0:T(1,128)S(1)} %bitcast.21), channel_id=1, replica_groups=mesh['dp'=4,'expert'=128] {'expert'}, dimensions={0} | all-to-all | bytes 131072 | tf_op jit(solution)/shard_map/all_to_all | solution.py:241
  258.9 0.0 copy-done.2
  258.9 0.0 copy-done.3
  258.9 0.0 copy-done.4
  258.9 0.7 shard_map.106
  259.7 0.0 collective-permute-done.far_ref
  259.7 0.0 collective-permute-done.1.ahead_ref
  259.7 0.0 collective-permute-done.2.behind_ref
  259.7 1.2 shard_map.105
Async XLA Ops:
  7.9 204.7 %copy-start = (bf16[1,2048,384]{2,1,0:T(8,128)(2,1)S(1)}, bf16[1,2048,384]{2,1,0:T(8,128)(2,1)}, u32[]{:S(2)}) copy-start(bf16[1,2048,384]{2,1,0:T(8,128)(2,1)} %param.14) | copy-start | bytes 4718596
  7.9 204.7 %copy-start.1 = (bf16[1,384,2048]{2,1,0:T(8,128)(2,1)S(1)}, bf16[1,384,2048]{2,1,0:T(8,128)(2,1)}, u32[]{:S(2)}) copy-start(bf16[1,384,2048]{2,1,0:T(8,128)(2,1)} %param.15) | copy-start | bytes 4718596
  7.9 204.7 %copy-start.5 = (s32[2]{0:T(128)S(1)}, s32[2]{0:T(128)}, u32[]{:S(2)}) copy-start(s32[2]{0:T(128)} %pad_add_fusion.place_ref) | copy-start | bytes 28
  212.6 46.3 %copy-start.2 = (f32[128,128]{1,0:T(8,128)S(1)}, f32[128,128]{1,0:T(8,128)}, u32[]{:S(2)}) copy-start(f32[128,128]{1,0:T(8,128)} %get-tuple-element.20.code_ref) | copy-start | bytes 196612
  212.6 46.3 %copy-start.3 = (s32[128,4]{0,1:T(4,128)S(1)}, s32[128,4]{0,1:T(4,128)}, u32[]{:S(2)}) copy-start(s32[128,4]{0,1:T(4,128)} %param.11) | copy-start | bytes 6148
  212.6 46.3 %copy-start.4 = (bf16[128,4]{0,1:T(4,128)(2,1)S(1)}, bf16[128,4]{0,1:T(4,128)(2,1)}, u32[]{:S(2)}) copy-start(bf16[128,4]{0,1:T(4,128)(2,1)} %param.10) | copy-start | bytes 3076
  219.1 40.6 %collective-permute-start = (bf16[3072,128]{1,0:T(8,128)(2,1)S(1)}, bf16[3072,128]{1,0:T(8,128)(2,1)S(1)}, u32[]{:S(2)}, u32[]{:S(2)}) collective-permute-start(bf16[3072,128]{1,0:T(8,128)(2,1)S(1)} %get-tuple-element.14), channel_id=1, source_target_pairs={{0,256},{128,384},{256,0},{384,128},{1,257},{129,385},{257,1},{385... | collective-permute-start | bytes 2359304 | tf_op jit(solution)/shard_map/ppermute | solution.py:228
  223.7 35.9 %collective-permute-start.1 = (bf16[3072,128]{1,0:T(8,128)(2,1)S(1)}, bf16[3072,128]{1,0:T(8,128)(2,1)S(1)}, u32[]{:S(2)}, u32[]{:S(2)}) collective-permute-start(bf16[3072,128]{1,0:T(8,128)(2,1)S(1)} %get-tuple-element.15), channel_id=1, source_target_pairs={{0,128},{128,256},{256,384},{384,0},{1,129},{129,257},{257,385},{3... | collective-permute-start | bytes 2359304 | tf_op jit(solution)/shard_map/ppermute | solution.py:228
  225.9 33.7 %collective-permute-start.2 = (bf16[3072,128]{1,0:T(8,128)(2,1)S(1)}, bf16[3072,128]{1,0:T(8,128)(2,1)S(1)}, u32[]{:S(2)}, u32[]{:S(2)}) collective-permute-start(bf16[3072,128]{1,0:T(8,128)(2,1)S(1)} %get-tuple-element.16), channel_id=1, source_target_pairs={{0,384},{128,0},{256,128},{384,256},{1,385},{129,1},{257,129},{385... | collective-permute-start | bytes 2359304 | tf_op jit(solution)/shard_map/ppermute | solution.py:228

commit v5 on v4

--- a/solution.py
+++ b/solution.py
@@ -8,6 +8,7 @@
 SLOTS = 4
 CHUNK = 2 * SLOTS
 LANES = 128
+STEPS = 1
 
 
 def contract(a, b, dims):
@@ -15,17 +16,17 @@
 
 
 def route_pack(
-    place_ref, ids_hbm, gates_hbm, hot_hbm, caps_hbm, x_hbm, dy_hbm, sent_hbm, code_ref,
-    ids_ref, gates_ref, hot_ref, caps_ref, x_ref, dy_ref, sent_ref, sems,
+    me_ref, odd_ref, ids_hbm, gates_hbm, hot_hbm, caps_hbm, x_hbm, dy_hbm, sent_hbm, code_ref,
+    ids_ref, gates_ref, hot_ref, caps_ref, rows_ref, sent_ref, sems,
 ):
+    top, count = ids_ref.shape
     pairs = (
-        (ids_hbm, ids_ref), (gates_hbm, gates_ref), (hot_hbm, hot_ref),
-        (caps_hbm, caps_ref), (x_hbm, x_ref), (dy_hbm, dy_ref),
+        (ids_hbm, ids_ref), (gates_hbm, gates_ref), (hot_hbm, hot_ref), (caps_hbm, caps_ref),
+        (x_hbm, rows_ref.at[pl.ds(0, count), :]), (dy_hbm, rows_ref.at[pl.ds(count, count), :]),
     )
     copies = [pltpu.make_async_copy(a, b, sems.at[i]) for i, (a, b) in enumerate(pairs)]
     for copy in copies:
         copy.start()
-    top, count = ids_ref.shape
     experts = hot_ref.shape[1]
     wide = experts * CHUNK
     lane = lax.broadcasted_iota(jnp.int32, (count, experts), 1).astype(jnp.float32)
@@ -56,7 +57,7 @@
         gate = jnp.where(hit, gates[:, at], gate)
     rank = contract(below, picked.astype(jnp.bfloat16), ((1,), (0,)))
     admitted = jnp.where(rank < caps_ref[...].astype(jnp.float32), picked, 0.0)
-    moves = hot_ref[...].astype(jnp.float32) * place_ref[1].astype(jnp.float32)
+    moves = hot_ref[...].astype(jnp.float32) * odd_ref[0].astype(jnp.float32)
     moved = admitted * moves
     stay = admitted - moved
     moved_next = pltpu.roll(moved, 1, 1)
@@ -70,21 +71,21 @@
     part = lax.broadcasted_iota(jnp.int32, (count, wide), 1) % CHUNK
     code_wide = contract(code, spread, ((1,), (0,)))
     gate_wide = contract(gate.astype(jnp.bfloat16), spread, ((1,), (0,)))
-    take_x = (code_wide == part.astype(jnp.float32)).astype(jnp.bfloat16)
     chosen = code_wide == (part - SLOTS).astype(jnp.float32)
-    take_dy = chosen.astype(jnp.bfloat16)
+    take = jnp.concatenate([code_wide == part.astype(jnp.float32), chosen], axis=0).astype(jnp.bfloat16)
     gate_pick = jnp.where(chosen, gate_wide, 0.0).astype(jnp.bfloat16)
     ones = jnp.ones((count, LANES), jnp.bfloat16)
-    gate_col = contract(gate_pick, ones, ((0,), (0,)))
-    gate_col = jnp.concatenate([gate_col] * 4, axis=1)
-    step = gate_col.shape[1]
+    scale = contract(gate_pick, ones, ((0,), (0,)))
+    is_x = lax.broadcasted_iota(jnp.int32, (wide, LANES), 0) % CHUNK < SLOTS
+    scale = jnp.where(is_x, 1.0, scale)
+    scale = jnp.concatenate([scale] * 4, axis=1)
+    step = scale.shape[1]
     for copy in copies[4:]:
         copy.wait()
-    for c in range(x_ref.shape[1] // step):
+    for c in range(rows_ref.shape[1] // step):
         at = slice(c * step, (c + 1) * step)
-        rows_x = contract(take_x, x_ref[:, at], ((0,), (0,)))
-        rows_dy = contract(take_dy, dy_ref[:, at], ((0,), (0,)))
-        sent_ref[:, at] = (rows_x + gate_col * rows_dy).astype(jnp.bfloat16)
+        rows = contract(take, rows_ref[:, at], ((0,), (0,)))
+        sent_ref[:, at] = (rows * scale).astype(jnp.bfloat16)
         copies.append(pltpu.make_async_copy(sent_ref.at[:, at], sent_hbm.at[:, at], sems.at[6 + c]))
         copies[-1].start()
     for copy in copies[6:]:
@@ -106,15 +107,15 @@
 
 
 def expert_rows(
-    place_ref, recv_ref, up_ref, down_ref, own_ref, ahead_ref, behind_ref, far_ref, dot_ref,
+    me_ref, recv_ref, up_ref, down_ref, own_ref, ahead_ref, behind_ref, far_ref, dot_ref,
     x_ref, s_ref, hid_ref, pre_ref,
 ):
     half, width = x_ref.shape
-    step = half // 4
+    step = half // STEPS
     lower = lax.broadcasted_iota(jnp.int32, (step, width), 0) % CHUNK < SLOTS
     lane = lax.broadcasted_iota(jnp.int32, (step, LANES), 1)
     sub = lax.broadcasted_iota(jnp.int32, (step, LANES), 0) % CHUNK
-    for r in range(4):
+    for r in range(STEPS):
         at = slice(r * step, (r + 1) * step)
         first = recv_ref[at, :]
         second = recv_ref[r * step + half : (r + 1) * step + half, :]
@@ -133,10 +134,10 @@
         spread = jnp.where(lane == sub, dots, 0.0).reshape(groups, CHUNK, LANES)
         spread = jnp.sum(spread, axis=1)
         dot_ref[r * groups : (r + 1) * groups, :] = spread
-        dot_ref[(r + 4) * groups : (r + 5) * groups, :] = pltpu.roll(spread, LANES - SLOTS, 1)
+        dot_ref[(r + STEPS) * groups : (r + STEPS + 1) * groups, :] = pltpu.roll(spread, LANES - SLOTS, 1)
     parts = width * pre_ref.shape[1] * 2 // (own_ref.shape[0] * LANES)
     for shift, out_ref in ((2, far_ref), (1, ahead_ref), (3, behind_ref), (0, own_ref)):
-        write_piece(lax.rem(place_ref[0] + shift, parts), x_ref, s_ref, hid_ref, pre_ref, out_ref)
+        write_piece(lax.rem(me_ref[0] + shift, parts), x_ref, s_ref, hid_ref, pre_ref, out_ref)
 
 
 def add_pieces(own_ref, far_ref, ahead_ref, behind_ref, up_ref, down_ref):
@@ -182,7 +183,8 @@
     half = total // 2
     ids_t = expert_ids.T
     gates_t = gate_values.T
-    place = jnp.stack([lax.axis_index("dp"), lax.axis_index("expert") % 2]).astype(jnp.int32)
+    me = lax.axis_index("dp").astype(jnp.int32).reshape(1)
+    odd = (lax.axis_index("expert") % 2).astype(jnp.int32).reshape(1)
     whole = pltpu.CompilerParams(vmem_limit_bytes=56 << 20)
     part = pltpu.CompilerParams(vmem_limit_bytes=24 << 20)
     sent, code = pl.pallas_call(
@@ -191,20 +193,19 @@
             jax.ShapeDtypeStruct((total, width), jnp.bfloat16),
             jax.ShapeDtypeStruct((experts, count), jnp.float32),
         ),
-        in_specs=[SMEM] + [ANY] * 6,
+        in_specs=[SMEM, SMEM] + [ANY] * 6,
         out_specs=(ANY, VMEM),
         scratch_shapes=[
             pltpu.VMEM((top, count), jnp.int32),
             pltpu.VMEM((top, count), jnp.bfloat16),
             pltpu.VMEM((1, experts), jnp.int32),
             pltpu.VMEM((1, experts), jnp.int32),
-            pltpu.VMEM((count, width), jnp.bfloat16),
-            pltpu.VMEM((count, width), jnp.bfloat16),
+            pltpu.VMEM((2 * count, width), jnp.bfloat16),
             pltpu.VMEM((total, width), jnp.bfloat16),
             pltpu.SemaphoreType.DMA((6 + width // 512,)),
         ],
         compiler_params=whole,
-    )(place, ids_t, gates_t, hot_plan.reshape(1, -1), expert_caps.reshape(1, -1), tokens, cotangent)
+    )(me, odd, ids_t, gates_t, hot_plan.reshape(1, -1), expert_caps.reshape(1, -1), tokens, cotangent)
     recv = lax.all_to_all(
         sent.reshape(experts, CHUNK, width), "expert", split_axis=0, concat_axis=0, tiled=True
     )
@@ -222,7 +223,7 @@
             pltpu.VMEM((half, hidden_width), jnp.bfloat16),
         ],
         compiler_params=part,
-    )(place, recv.reshape(total, width), w_up[0], w_down[0])
+    )(me, recv.reshape(total, width), w_up[0], w_down[0])
 
     def shift(block, distance):
         return lax.ppermute(block, "dp", [(i, (i + distance) % groups) for i in range(groups)])

time: 263 us -> 259 us (0.985)
  Pallas kernels: 15 us -> 11.8 us
where the time goes in v5:
time: 259 us; the launch traced here: 257 us
  blocking collectives  233 us (90%)
  Pallas kernels  11.8 us (5%)
  starting transfers between devices  11.1 us (4%)
    all_to_all x1, blocking collectives, shards(): lax.all_to_all(sent.reshape(experts, CHUNK, width), 'expert', split_axis=...  205 us
    all_to_all x1, blocking collectives, shards(): lax.all_to_all(dots.reshape(experts, 1, LANES), 'expert', split_axis=0, c...  28.7 us
    ppermute x3, starting transfers between devices, shift(): lax.ppermute(block, 'dp', [(i, (i + distance) % groups) for i in range(gr...  11.1 us
  transfers between devices with their start and end apart: 3, of which 0 were waited for; matrix products, arithmetic and copies ran while one was open for 0% of the time, Pallas kernels for 0%

profile of v5, /device:TPU:1, one launch (start us, length us, event | category | flops | bytes accessed | tf_op | source)
XLA Modules:
  0.0 257.0 jit_solution(4548005053267637595)
XLA Ops:
  0.6 5.1 %shard_map.103 = (bf16[1024,2048]{1,0:T(8,128)(2,1)}, f32[128,128]{1,0:T(8,128)}) custom-call(s32[1]{0:T(128)} %bitcast.me_ref, s32[1]{0:T(128)} %bitcast.1.odd_ref, s32[4,128]{1,0:T(4,128)} %bitcast.22, bf16[4,128]{1,0:T(4,128)(2,1)} %bitcast.24, s32[1,128]{1,0:T(1,128)} %bitcast.28, s32[1,128]{1,0:T(1,128)} %bitcast.29, bf16[128,2048]{1,0:T(8,128)(2,1)} %x_hbm.1, ...), custom_call_target="tpu_custom_call" | custom-call | tf_op jit(solution)/shard_map/pallas_call | solution.py:190
  5.7 0.0 copy-start
  5.8 0.0 copy-start.1
  5.8 204.7 %all_to_all.10 = bf16[128,8,2048]{2,1,0:T(8,128)(2,1)S(1)} all-to-all(bf16[128,8,2048]{2,1,0:T(8,128)(2,1)} %bitcast.26), channel_id=1, replica_groups=mesh['dp'=4,'expert'=128] {'expert'}, dimensions={0} | all-to-all | bytes 8388608 | tf_op jit(solution)/shard_map/all_to_all | solution.py:209
  210.5 0.0 copy-start.2
  210.5 0.0 copy-start.3
  210.5 0.0 copy-start.4
  210.5 0.0 copy-done
  210.5 0.0 copy-done.1
  210.5 4.8 %shard_map.104 = (bf16[3072,128]{1,0:T(8,128)(2,1)S(1)}, bf16[3072,128]{1,0:T(8,128)(2,1)S(1)}, bf16[3072,128]{1,0:T(8,128)(2,1)S(1)}, bf16[3072,128]{1,0:T(8,128)(2,1)S(1)}, f32[128,128]{1,0:T(8,128)S(1)}) custom-call(s32[1]{0:T(128)} %bitcast.me_ref, bf16[1024,2048]{1,0:T(8,128)(2,1)S(1)} %bitcast.17, bf16[2048,384]{1,0:T(8,128)(2,1)S(1)} %bitcast.18, ...), custom_call_target="tpu_custom_call" | custom-call | tf_op jit(solution)/shard_map/pallas_call | solution.py:214
  215.3 4.6 %collective-permute-start = (bf16[3072,128]{1,0:T(8,128)(2,1)S(1)}, bf16[3072,128]{1,0:T(8,128)(2,1)S(1)}, u32[]{:S(2)}, u32[]{:S(2)}) collective-permute-start(bf16[3072,128]{1,0:T(8,128)(2,1)S(1)} %get-tuple-element.14), channel_id=1, source_target_pairs={{0,256},{128,384},{256,0},{384,128},{1,257},{129,385},{257,1},{385... | collective-permute-start | bytes 2359304 | tf_op jit(solution)/shard_map/ppermute | solution.py:229
  219.9 2.1 collective-permute-start.1
  222.1 4.3 %collective-permute-start.2 = (bf16[3072,128]{1,0:T(8,128)(2,1)S(1)}, bf16[3072,128]{1,0:T(8,128)(2,1)S(1)}, u32[]{:S(2)}, u32[]{:S(2)}) collective-permute-start(bf16[3072,128]{1,0:T(8,128)(2,1)S(1)} %get-tuple-element.16), channel_id=1, source_target_pairs={{0,384},{128,0},{256,128},{384,256},{1,385},{129,1},{257,129},{385... | collective-permute-start | bytes 2359304 | tf_op jit(solution)/shard_map/ppermute | solution.py:229
  226.4 28.7 %all_to_all.11 = f32[128,1,128]{2,1,0:T(1,128)S(1)} all-to-all(f32[128,1,128]{2,1,0:T(1,128)S(1)} %bitcast.21), channel_id=1, replica_groups=mesh['dp'=4,'expert'=128] {'expert'}, dimensions={0} | all-to-all | bytes 131072 | tf_op jit(solution)/shard_map/all_to_all | solution.py:242
  255.1 0.0 copy-done.2
  255.1 0.0 copy-done.3
  255.1 0.0 copy-done.4
  255.1 0.7 shard_map.106
  255.8 0.0 collective-permute-done.far_ref
  255.8 0.0 collective-permute-done.1.ahead_ref
  255.8 0.0 collective-permute-done.2.behind_ref
  255.9 1.2 shard_map.105
Async XLA Ops:
  5.7 204.7 %copy-start = (bf16[1,2048,384]{2,1,0:T(8,128)(2,1)S(1)}, bf16[1,2048,384]{2,1,0:T(8,128)(2,1)}, u32[]{:S(2)}) copy-start(bf16[1,2048,384]{2,1,0:T(8,128)(2,1)} %param.14) | copy-start | bytes 4718596
  5.8 204.7 %copy-start.1 = (bf16[1,384,2048]{2,1,0:T(8,128)(2,1)S(1)}, bf16[1,384,2048]{2,1,0:T(8,128)(2,1)}, u32[]{:S(2)}) copy-start(bf16[1,384,2048]{2,1,0:T(8,128)(2,1)} %param.15) | copy-start | bytes 4718596
  210.5 44.6 %copy-start.2 = (f32[128,128]{1,0:T(8,128)S(1)}, f32[128,128]{1,0:T(8,128)}, u32[]{:S(2)}) copy-start(f32[128,128]{1,0:T(8,128)} %get-tuple-element.20.code_ref) | copy-start | bytes 196612
  210.5 44.6 %copy-start.3 = (s32[128,4]{0,1:T(4,128)S(1)}, s32[128,4]{0,1:T(4,128)}, u32[]{:S(2)}) copy-start(s32[128,4]{0,1:T(4,128)} %param.11) | copy-start | bytes 6148
  210.5 44.6 %copy-start.4 = (bf16[128,4]{0,1:T(4,128)(2,1)S(1)}, bf16[128,4]{0,1:T(4,128)(2,1)}, u32[]{:S(2)}) copy-start(bf16[128,4]{0,1:T(4,128)(2,1)} %param.10) | copy-start | bytes 3076
  215.3 40.6 %collective-permute-start = (bf16[3072,128]{1,0:T(8,128)(2,1)S(1)}, bf16[3072,128]{1,0:T(8,128)(2,1)S(1)}, u32[]{:S(2)}, u32[]{:S(2)}) collective-permute-start(bf16[3072,128]{1,0:T(8,128)(2,1)S(1)} %get-tuple-element.14), channel_id=1, source_target_pairs={{0,256},{128,384},{256,0},{384,128},{1,257},{129,385},{257,1},{385... | collective-permute-start | bytes 2359304 | tf_op jit(solution)/shard_map/ppermute | solution.py:229
  219.9 35.9 %collective-permute-start.1 = (bf16[3072,128]{1,0:T(8,128)(2,1)S(1)}, bf16[3072,128]{1,0:T(8,128)(2,1)S(1)}, u32[]{:S(2)}, u32[]{:S(2)}) collective-permute-start(bf16[3072,128]{1,0:T(8,128)(2,1)S(1)} %get-tuple-element.15), channel_id=1, source_target_pairs={{0,128},{128,256},{256,384},{384,0},{1,129},{129,257},{257,385},{3... | collective-permute-start | bytes 2359304 | tf_op jit(solution)/shard_map/ppermute | solution.py:229
  222.1 33.8 %collective-permute-start.2 = (bf16[3072,128]{1,0:T(8,128)(2,1)S(1)}, bf16[3072,128]{1,0:T(8,128)(2,1)S(1)}, u32[]{:S(2)}, u32[]{:S(2)}) collective-permute-start(bf16[3072,128]{1,0:T(8,128)(2,1)S(1)} %get-tuple-element.16), channel_id=1, source_target_pairs={{0,384},{128,0},{256,128},{384,256},{1,385},{129,1},{257,129},{385... | collective-permute-start | bytes 2359304 | tf_op jit(solution)/shard_map/ppermute | solution.py:229

commit v6 on v5

--- a/solution.py
+++ b/solution.py
@@ -71,21 +71,16 @@
     part = lax.broadcasted_iota(jnp.int32, (count, wide), 1) % CHUNK
     code_wide = contract(code, spread, ((1,), (0,)))
     gate_wide = contract(gate.astype(jnp.bfloat16), spread, ((1,), (0,)))
-    chosen = code_wide == (part - SLOTS).astype(jnp.float32)
-    take = jnp.concatenate([code_wide == part.astype(jnp.float32), chosen], axis=0).astype(jnp.bfloat16)
-    gate_pick = jnp.where(chosen, gate_wide, 0.0).astype(jnp.bfloat16)
-    ones = jnp.ones((count, LANES), jnp.bfloat16)
-    scale = contract(gate_pick, ones, ((0,), (0,)))
-    is_x = lax.broadcasted_iota(jnp.int32, (wide, LANES), 0) % CHUNK < SLOTS
-    scale = jnp.where(is_x, 1.0, scale)
-    scale = jnp.concatenate([scale] * 4, axis=1)
-    step = scale.shape[1]
+    put = jnp.where(code_wide == (part - SLOTS).astype(jnp.float32), gate_wide, 0.0)
+    take = jnp.concatenate([(code_wide == part.astype(jnp.float32)).astype(jnp.float32), put], axis=0)
+    take = take.astype(jnp.bfloat16)
+    step = 4 * LANES
     for copy in copies[4:]:
         copy.wait()
     for c in range(rows_ref.shape[1] // step):
         at = slice(c * step, (c + 1) * step)
         rows = contract(take, rows_ref[:, at], ((0,), (0,)))
-        sent_ref[:, at] = (rows * scale).astype(jnp.bfloat16)
+        sent_ref[:, at] = rows.astype(jnp.bfloat16)
         copies.append(pltpu.make_async_copy(sent_ref.at[:, at], sent_hbm.at[:, at], sems.at[6 + c]))
         copies[-1].start()
     for copy in copies[6:]:
@@ -123,8 +118,8 @@
         s = jnp.where(lower, pltpu.roll(first, step - SLOTS, 0), second)
         x_ref[at, :] = x
         s_ref[at, :] = s
+        backprop = contract(s, down_ref[...], ((1,), (1,)))
         preact = contract(x, up_ref[...], ((1,), (0,)))
-        backprop = contract(s, down_ref[...], ((1,), (1,)))
         sigma = jax.nn.sigmoid(preact)
         hidden = (preact * sigma).astype(jnp.bfloat16)
         hid_ref[:, at] = hidden.T

time: 259 us -> 259 us (level)
  no operation moved by 1% of the time
where the time goes in v6:
time: 259 us; the launch traced here: 257 us
  blocking collectives  233 us (90%)
  Pallas kernels  11.4 us (4%)
  starting transfers between devices  11.1 us (4%)
    all_to_all x1, blocking collectives, shards(): lax.all_to_all(sent.reshape(experts, CHUNK, width), 'expert', split_axis=...  205 us
    all_to_all x1, blocking collectives, shards(): lax.all_to_all(dots.reshape(experts, 1, LANES), 'expert', split_axis=0, c...  28.7 us
    ppermute x3, starting transfers between devices, shift(): lax.ppermute(block, 'dp', [(i, (i + distance) % groups) for i in range(gr...  11.1 us
  transfers between devices with their start and end apart: 3, of which 0 were waited for; matrix products, arithmetic and copies ran while one was open for 0% of the time, Pallas kernels for 0%

profile of v6, /device:TPU:1, one launch (start us, length us, event | category | flops | bytes accessed | tf_op | source)
XLA Modules:
  0.0 256.6 jit_solution(18113520003087851151)
XLA Ops:
  0.6 4.9 %shard_map.103 = (bf16[1024,2048]{1,0:T(8,128)(2,1)}, f32[128,128]{1,0:T(8,128)}) custom-call(s32[1]{0:T(128)} %bitcast.me_ref, s32[1]{0:T(128)} %bitcast.1.odd_ref, s32[4,128]{1,0:T(4,128)} %bitcast.22, bf16[4,128]{1,0:T(4,128)(2,1)} %bitcast.24, s32[1,128]{1,0:T(1,128)} %bitcast.28, s32[1,128]{1,0:T(1,128)} %bitcast.29, bf16[128,2048]{1,0:T(8,128)(2,1)} %x_hbm.1, ...), custom_call_target="tpu_custom_call" | custom-call | tf_op jit(solution)/shard_map/pallas_call | solution.py:185
  5.5 0.0 copy-start
  5.5 0.0 copy-start.1
  5.6 204.7 %all_to_all.10 = bf16[128,8,2048]{2,1,0:T(8,128)(2,1)S(1)} all-to-all(bf16[128,8,2048]{2,1,0:T(8,128)(2,1)} %bitcast.26), channel_id=1, replica_groups=mesh['dp'=4,'expert'=128] {'expert'}, dimensions={0} | all-to-all | bytes 8388608 | tf_op jit(solution)/shard_map/all_to_all | solution.py:204
  210.3 0.0 copy-start.2
  210.3 0.0 copy-start.3
  210.3 0.0 copy-start.4
  210.3 0.0 copy-done
  210.3 0.0 copy-done.1
  210.3 4.6 %shard_map.104 = (bf16[3072,128]{1,0:T(8,128)(2,1)S(1)}, bf16[3072,128]{1,0:T(8,128)(2,1)S(1)}, bf16[3072,128]{1,0:T(8,128)(2,1)S(1)}, bf16[3072,128]{1,0:T(8,128)(2,1)S(1)}, f32[128,128]{1,0:T(8,128)S(1)}) custom-call(s32[1]{0:T(128)} %bitcast.me_ref, bf16[1024,2048]{1,0:T(8,128)(2,1)S(1)} %bitcast.17, bf16[2048,384]{1,0:T(8,128)(2,1)S(1)} %bitcast.18, ...), custom_call_target="tpu_custom_call" | custom-call | tf_op jit(solution)/shard_map/pallas_call | solution.py:209
  214.9 4.7 %collective-permute-start = (bf16[3072,128]{1,0:T(8,128)(2,1)S(1)}, bf16[3072,128]{1,0:T(8,128)(2,1)S(1)}, u32[]{:S(2)}, u32[]{:S(2)}) collective-permute-start(bf16[3072,128]{1,0:T(8,128)(2,1)S(1)} %get-tuple-element.14), channel_id=1, source_target_pairs={{0,256},{128,384},{256,0},{384,128},{1,257},{129,385},{257,1},{385... | collective-permute-start | bytes 2359304 | tf_op jit(solution)/shard_map/ppermute | solution.py:224
  219.5 2.2 collective-permute-start.1
  221.7 4.3 %collective-permute-start.2 = (bf16[3072,128]{1,0:T(8,128)(2,1)S(1)}, bf16[3072,128]{1,0:T(8,128)(2,1)S(1)}, u32[]{:S(2)}, u32[]{:S(2)}) collective-permute-start(bf16[3072,128]{1,0:T(8,128)(2,1)S(1)} %get-tuple-element.16), channel_id=1, source_target_pairs={{0,384},{128,0},{256,128},{384,256},{1,385},{129,1},{257,129},{385... | collective-permute-start | bytes 2359304 | tf_op jit(solution)/shard_map/ppermute | solution.py:224
  226.0 28.7 %all_to_all.11 = f32[128,1,128]{2,1,0:T(1,128)S(1)} all-to-all(f32[128,1,128]{2,1,0:T(1,128)S(1)} %bitcast.21), channel_id=1, replica_groups=mesh['dp'=4,'expert'=128] {'expert'}, dimensions={0} | all-to-all | bytes 131072 | tf_op jit(solution)/shard_map/all_to_all | solution.py:237
  254.7 0.0 copy-done.2
  254.7 0.0 copy-done.3
  254.7 0.0 copy-done.4
  254.7 0.7 shard_map.106
  255.5 0.0 collective-permute-done.far_ref
  255.5 0.0 collective-permute-done.1.ahead_ref
  255.5 0.0 collective-permute-done.2.behind_ref
  255.5 1.2 shard_map.105
Async XLA Ops:
  5.5 204.7 %copy-start = (bf16[1,2048,384]{2,1,0:T(8,128)(2,1)S(1)}, bf16[1,2048,384]{2,1,0:T(8,128)(2,1)}, u32[]{:S(2)}) copy-start(bf16[1,2048,384]{2,1,0:T(8,128)(2,1)} %param.14) | copy-start | bytes 4718596
  5.5 204.7 %copy-start.1 = (bf16[1,384,2048]{2,1,0:T(8,128)(2,1)S(1)}, bf16[1,384,2048]{2,1,0:T(8,128)(2,1)}, u32[]{:S(2)}) copy-start(bf16[1,384,2048]{2,1,0:T(8,128)(2,1)} %param.15) | copy-start | bytes 4718596
  210.3 44.5 %copy-start.2 = (f32[128,128]{1,0:T(8,128)S(1)}, f32[128,128]{1,0:T(8,128)}, u32[]{:S(2)}) copy-start(f32[128,128]{1,0:T(8,128)} %get-tuple-element.20.code_ref) | copy-start | bytes 196612
  210.3 44.5 %copy-start.3 = (s32[128,4]{0,1:T(4,128)S(1)}, s32[128,4]{0,1:T(4,128)}, u32[]{:S(2)}) copy-start(s32[128,4]{0,1:T(4,128)} %param.11) | copy-start | bytes 6148
  210.3 44.5 %copy-start.4 = (bf16[128,4]{0,1:T(4,128)(2,1)S(1)}, bf16[128,4]{0,1:T(4,128)(2,1)}, u32[]{:S(2)}) copy-start(bf16[128,4]{0,1:T(4,128)(2,1)} %param.10) | copy-start | bytes 3076
  214.9 40.6 %collective-permute-start = (bf16[3072,128]{1,0:T(8,128)(2,1)S(1)}, bf16[3072,128]{1,0:T(8,128)(2,1)S(1)}, u32[]{:S(2)}, u32[]{:S(2)}) collective-permute-start(bf16[3072,128]{1,0:T(8,128)(2,1)S(1)} %get-tuple-element.14), channel_id=1, source_target_pairs={{0,256},{128,384},{256,0},{384,128},{1,257},{129,385},{257,1},{385... | collective-permute-start | bytes 2359304 | tf_op jit(solution)/shard_map/ppermute | solution.py:224
  219.5 35.9 %collective-permute-start.1 = (bf16[3072,128]{1,0:T(8,128)(2,1)S(1)}, bf16[3072,128]{1,0:T(8,128)(2,1)S(1)}, u32[]{:S(2)}, u32[]{:S(2)}) collective-permute-start(bf16[3072,128]{1,0:T(8,128)(2,1)S(1)} %get-tuple-element.15), channel_id=1, source_target_pairs={{0,128},{128,256},{256,384},{384,0},{1,129},{129,257},{257,385},{3... | collective-permute-start | bytes 2359304 | tf_op jit(solution)/shard_map/ppermute | solution.py:224
  221.7 33.7 %collective-permute-start.2 = (bf16[3072,128]{1,0:T(8,128)(2,1)S(1)}, bf16[3072,128]{1,0:T(8,128)(2,1)S(1)}, u32[]{:S(2)}, u32[]{:S(2)}) collective-permute-start(bf16[3072,128]{1,0:T(8,128)(2,1)S(1)} %get-tuple-element.16), channel_id=1, source_target_pairs={{0,384},{128,0},{256,128},{384,256},{1,385},{129,1},{257,129},{385... | collective-permute-start | bytes 2359304 | tf_op jit(solution)/shard_map/ppermute | solution.py:224

commit v7 on v6

--- a/solution.py
+++ b/solution.py
@@ -131,11 +131,11 @@
         dot_ref[r * groups : (r + 1) * groups, :] = spread
         dot_ref[(r + STEPS) * groups : (r + STEPS + 1) * groups, :] = pltpu.roll(spread, LANES - SLOTS, 1)
     parts = width * pre_ref.shape[1] * 2 // (own_ref.shape[0] * LANES)
-    for shift, out_ref in ((2, far_ref), (1, ahead_ref), (3, behind_ref), (0, own_ref)):
+    for shift, out_ref in ((1, ahead_ref), (3, behind_ref), (2, far_ref), (0, own_ref)):
         write_piece(lax.rem(me_ref[0] + shift, parts), x_ref, s_ref, hid_ref, pre_ref, out_ref)
 
 
-def add_pieces(own_ref, far_ref, ahead_ref, behind_ref, up_ref, down_ref):
+def add_pieces(own_ref, ahead_ref, behind_ref, far_ref, up_ref, down_ref):
     refs = (own_ref, far_ref, ahead_ref, behind_ref)
     wide, tall = up_ref.shape
     base = wide * tall // LANES
@@ -223,7 +223,7 @@
     def shift(block, distance):
         return lax.ppermute(block, "dp", [(i, (i + distance) % groups) for i in range(groups)])
 
-    far, ahead, behind = shift(far, 2), shift(ahead, 1), shift(behind, 3)
+    ahead, behind, far = shift(ahead, 1), shift(behind, 3), shift(far, 2)
     summed_up, summed_down = pl.pallas_call(
         add_pieces,
         out_shape=(
@@ -233,7 +233,7 @@
         in_specs=[VMEM] * 4,
         out_specs=(VMEM,) * 2,
         compiler_params=pltpu.CompilerParams(vmem_limit_bytes=12 << 20),
-    )(own, far, ahead, behind)
+    )(own, ahead, behind, far)
     back = lax.all_to_all(
         dots.reshape(experts, 1, LANES), "expert", split_axis=0, concat_axis=0, tiled=True
     )

time: 259 us -> 261 us (level)
  the two profiles are of different devices: /device:TPU:1 before, /device:TPU:90 now
where the time goes in v7:
time: 261 us; the launch traced here: 260 us
  blocking collectives  227 us (87%)
  Pallas kernels  11.3 us (4%)
  waiting for transfers between devices  10.9 us (4%)
  starting transfers between devices  9.88 us (4%)
    all_to_all x1, blocking collectives, shards(): lax.all_to_all(sent.reshape(experts, CHUNK, width), 'expert', split_axis=...  207 us
    all_to_all x1, blocking collectives, shards(): lax.all_to_all(dots.reshape(experts, 1, LANES), 'expert', split_axis=0, c...  20.3 us
    ppermute x3, waiting for transfers between devices, shift(): lax.ppermute(block, 'dp', [(i, (i + distance) % groups) for i in range(gr...  10.9 us
    ppermute x3, starting transfers between devices, shift(): lax.ppermute(block, 'dp', [(i, (i + distance) % groups) for i in range(gr...  9.88 us
  transfers between devices with their start and end apart: 3, of which 1 were waited for; matrix products, arithmetic and copies ran while one was open for 0% of the time, Pallas kernels for 0%

profile of v7, /device:TPU:90, one launch (start us, length us, event | category | flops | bytes accessed | tf_op | source)
XLA Modules:
  0.0 260.3 jit_solution(5239659996451469892)
XLA Ops:
  0.6 4.9 %shard_map.103 = (bf16[1024,2048]{1,0:T(8,128)(2,1)}, f32[128,128]{1,0:T(8,128)}) custom-call(s32[1]{0:T(128)} %bitcast.me_ref, s32[1]{0:T(128)} %bitcast.1.odd_ref, s32[4,128]{1,0:T(4,128)} %bitcast.22, bf16[4,128]{1,0:T(4,128)(2,1)} %bitcast.24, s32[1,128]{1,0:T(1,128)} %bitcast.28, s32[1,128]{1,0:T(1,128)} %bitcast.29, bf16[128,2048]{1,0:T(8,128)(2,1)} %x_hbm.1, ...), custom_call_target="tpu_custom_call" | custom-call | tf_op jit(solution)/shard_map/pallas_call | solution.py:185
  5.5 0.0 copy-start
  5.5 0.0 copy-start.1
  5.6 207.1 %all_to_all.10 = bf16[128,8,2048]{2,1,0:T(8,128)(2,1)S(1)} all-to-all(bf16[128,8,2048]{2,1,0:T(8,128)(2,1)} %bitcast.26), channel_id=1, replica_groups=mesh['dp'=4,'expert'=128] {'expert'}, dimensions={0} | all-to-all | bytes 8388608 | tf_op jit(solution)/shard_map/all_to_all | solution.py:204
  212.7 0.0 copy-start.2
  212.7 0.0 copy-start.3
  212.7 0.0 copy-start.4
  212.7 0.0 copy-done
  212.7 0.0 copy-done.1
  212.7 4.6 %shard_map.104 = (bf16[3072,128]{1,0:T(8,128)(2,1)S(1)}, bf16[3072,128]{1,0:T(8,128)(2,1)S(1)}, bf16[3072,128]{1,0:T(8,128)(2,1)S(1)}, bf16[3072,128]{1,0:T(8,128)(2,1)S(1)}, f32[128,128]{1,0:T(8,128)S(1)}) custom-call(s32[1]{0:T(128)} %bitcast.me_ref, bf16[1024,2048]{1,0:T(8,128)(2,1)S(1)} %bitcast.17, bf16[2048,384]{1,0:T(8,128)(2,1)S(1)} %bitcast.18, ...), custom_call_target="tpu_custom_call" | custom-call | tf_op jit(solution)/shard_map/pallas_call | solution.py:209
  217.3 3.4 %collective-permute-start = (bf16[3072,128]{1,0:T(8,128)(2,1)S(1)}, bf16[3072,128]{1,0:T(8,128)(2,1)S(1)}, u32[]{:S(2)}, u32[]{:S(2)}) collective-permute-start(bf16[3072,128]{1,0:T(8,128)(2,1)S(1)} %get-tuple-element.14), channel_id=1, source_target_pairs={{0,128},{128,256},{256,384},{384,0},{1,129},{129,257},{257,385},{3... | collective-permute-start | bytes 2359304 | tf_op jit(solution)/shard_map/ppermute | solution.py:224
  220.7 2.4 collective-permute-start.1
  223.1 4.0 %collective-permute-start.2 = (bf16[3072,128]{1,0:T(8,128)(2,1)S(1)}, bf16[3072,128]{1,0:T(8,128)(2,1)S(1)}, u32[]{:S(2)}, u32[]{:S(2)}) collective-permute-start(bf16[3072,128]{1,0:T(8,128)(2,1)S(1)} %get-tuple-element.16), channel_id=1, source_target_pairs={{0,256},{128,384},{256,0},{384,128},{1,257},{129,385},{257,1},{385... | collective-permute-start | bytes 2359304 | tf_op jit(solution)/shard_map/ppermute | solution.py:224
  227.2 20.3 %all_to_all.11 = f32[128,1,128]{2,1,0:T(1,128)S(1)} all-to-all(f32[128,1,128]{2,1,0:T(1,128)S(1)} %bitcast.21), channel_id=1, replica_groups=mesh['dp'=4,'expert'=128] {'expert'}, dimensions={0} | all-to-all | bytes 131072 | tf_op jit(solution)/shard_map/all_to_all | solution.py:237
  247.5 0.0 copy-done.2
  247.5 0.0 copy-done.3
  247.5 0.0 copy-done.4
  247.5 0.7 shard_map.106
  248.3 0.0 collective-permute-done.ahead_ref
  248.3 0.0 collective-permute-done.1.behind_ref
  248.3 10.9 %collective-permute-done.2.far_ref = bf16[3072,128]{1,0:T(8,128)(2,1)S(1)} collective-permute-done((bf16[3072,128]{1,0:T(8,128)(2,1)S(1)}, bf16[3072,128]{1,0:T(8,128)(2,1)S(1)}, u32[]{:S(2)}, u32[]{:S(2)}) %collective-permute-start.2) | collective-permute-done | bytes 786464 | tf_op jit(solution)/shard_map/ppermute | solution.py:224
  259.2 1.2 shard_map.105
Async XLA Ops:
  5.5 207.2 %copy-start = (bf16[1,2048,384]{2,1,0:T(8,128)(2,1)S(1)}, bf16[1,2048,384]{2,1,0:T(8,128)(2,1)}, u32[]{:S(2)}) copy-start(bf16[1,2048,384]{2,1,0:T(8,128)(2,1)} %param.14) | copy-start | bytes 4718596
  5.5 207.2 %copy-start.1 = (bf16[1,384,2048]{2,1,0:T(8,128)(2,1)S(1)}, bf16[1,384,2048]{2,1,0:T(8,128)(2,1)}, u32[]{:S(2)}) copy-start(bf16[1,384,2048]{2,1,0:T(8,128)(2,1)} %param.15) | copy-start | bytes 4718596
  212.7 34.8 %copy-start.2 = (f32[128,128]{1,0:T(8,128)S(1)}, f32[128,128]{1,0:T(8,128)}, u32[]{:S(2)}) copy-start(f32[128,128]{1,0:T(8,128)} %get-tuple-element.20.code_ref) | copy-start | bytes 196612
  212.7 34.8 %copy-start.3 = (s32[128,4]{0,1:T(4,128)S(1)}, s32[128,4]{0,1:T(4,128)}, u32[]{:S(2)}) copy-start(s32[128,4]{0,1:T(4,128)} %param.11) | copy-start | bytes 6148
  212.7 34.8 %copy-start.4 = (bf16[128,4]{0,1:T(4,128)(2,1)S(1)}, bf16[128,4]{0,1:T(4,128)(2,1)}, u32[]{:S(2)}) copy-start(bf16[128,4]{0,1:T(4,128)(2,1)} %param.10) | copy-start | bytes 3076
  217.3 31.0 %collective-permute-start = (bf16[3072,128]{1,0:T(8,128)(2,1)S(1)}, bf16[3072,128]{1,0:T(8,128)(2,1)S(1)}, u32[]{:S(2)}, u32[]{:S(2)}) collective-permute-start(bf16[3072,128]{1,0:T(8,128)(2,1)S(1)} %get-tuple-element.14), channel_id=1, source_target_pairs={{0,128},{128,256},{256,384},{384,0},{1,129},{129,257},{257,385},{3... | collective-permute-start | bytes 2359304 | tf_op jit(solution)/shard_map/ppermute | solution.py:224
  220.7 27.6 %collective-permute-start.1 = (bf16[3072,128]{1,0:T(8,128)(2,1)S(1)}, bf16[3072,128]{1,0:T(8,128)(2,1)S(1)}, u32[]{:S(2)}, u32[]{:S(2)}) collective-permute-start(bf16[3072,128]{1,0:T(8,128)(2,1)S(1)} %get-tuple-element.15), channel_id=1, source_target_pairs={{0,384},{128,0},{256,128},{384,256},{1,385},{129,1},{257,129},{385... | collective-permute-start | bytes 2359304 | tf_op jit(solution)/shard_map/ppermute | solution.py:224
  223.1 36.1 %collective-permute-start.2 = (bf16[3072,128]{1,0:T(8,128)(2,1)S(1)}, bf16[3072,128]{1,0:T(8,128)(2,1)S(1)}, u32[]{:S(2)}, u32[]{:S(2)}) collective-permute-start(bf16[3072,128]{1,0:T(8,128)(2,1)S(1)} %get-tuple-element.16), channel_id=1, source_target_pairs={{0,256},{128,384},{256,0},{384,128},{1,257},{129,385},{257,1},{385... | collective-permute-start | bytes 2359304 | tf_op jit(solution)/shard_map/ppermute | solution.py:224

commit v8 on v7

--- a/solution.py
+++ b/solution.py
@@ -131,11 +131,11 @@
         dot_ref[r * groups : (r + 1) * groups, :] = spread
         dot_ref[(r + STEPS) * groups : (r + STEPS + 1) * groups, :] = pltpu.roll(spread, LANES - SLOTS, 1)
     parts = width * pre_ref.shape[1] * 2 // (own_ref.shape[0] * LANES)
-    for shift, out_ref in ((1, ahead_ref), (3, behind_ref), (2, far_ref), (0, own_ref)):
+    for shift, out_ref in ((1, ahead_ref), (2, far_ref), (3, behind_ref), (0, own_ref)):
         write_piece(lax.rem(me_ref[0] + shift, parts), x_ref, s_ref, hid_ref, pre_ref, out_ref)
 
 
-def add_pieces(own_ref, ahead_ref, behind_ref, far_ref, up_ref, down_ref):
+def add_pieces(own_ref, ahead_ref, far_ref, behind_ref, up_ref, down_ref):
     refs = (own_ref, far_ref, ahead_ref, behind_ref)
     wide, tall = up_ref.shape
     base = wide * tall // LANES
@@ -223,7 +223,7 @@
     def shift(block, distance):
         return lax.ppermute(block, "dp", [(i, (i + distance) % groups) for i in range(groups)])
 
-    ahead, behind, far = shift(ahead, 1), shift(behind, 3), shift(far, 2)
+    ahead, far, behind = shift(ahead, 1), shift(far, 2), shift(behind, 3)
     summed_up, summed_down = pl.pallas_call(
         add_pieces,
         out_shape=(
@@ -233,7 +233,7 @@
         in_specs=[VMEM] * 4,
         out_specs=(VMEM,) * 2,
         compiler_params=pltpu.CompilerParams(vmem_limit_bytes=12 << 20),
-    )(own, ahead, behind, far)
+    )(own, ahead, far, behind)
     back = lax.all_to_all(
         dots.reshape(experts, 1, LANES), "expert", split_axis=0, concat_axis=0, tiled=True
     )

time: 261 us -> 262 us (level)
  the two profiles are of different devices: /device:TPU:90 before, /device:TPU:1 now
where the time goes in v8:
time: 262 us; the launch traced here: 257 us
  blocking collectives  233 us (89%)
  Pallas kernels  11.3 us (4%)
  starting transfers between devices  10.5 us (4%)
    all_to_all x1, blocking collectives, shards(): lax.all_to_all(sent.reshape(experts, CHUNK, width), 'expert', split_axis=...  205 us
    all_to_all x1, blocking collectives, shards(): lax.all_to_all(dots.reshape(experts, 1, LANES), 'expert', split_axis=0, c...  28.7 us
    ppermute x3, starting transfers between devices, shift(): lax.ppermute(block, 'dp', [(i, (i + distance) % groups) for i in range(gr...  10.5 us
  transfers between devices with their start and end apart: 3, of which 1 were waited for; matrix products, arithmetic and copies ran while one was open for 0% of the time, Pallas kernels for 0%

profile of v8, /device:TPU:1, one launch (start us, length us, event | category | flops | bytes accessed | tf_op | source)
XLA Modules:
  0.0 256.9 jit_solution(313938015740657111)
XLA Ops:
  0.6 4.9 %shard_map.103 = (bf16[1024,2048]{1,0:T(8,128)(2,1)}, f32[128,128]{1,0:T(8,128)}) custom-call(s32[1]{0:T(128)} %bitcast.me_ref, s32[1]{0:T(128)} %bitcast.1.odd_ref, s32[4,128]{1,0:T(4,128)} %bitcast.22, bf16[4,128]{1,0:T(4,128)(2,1)} %bitcast.24, s32[1,128]{1,0:T(1,128)} %bitcast.28, s32[1,128]{1,0:T(1,128)} %bitcast.29, bf16[128,2048]{1,0:T(8,128)(2,1)} %x_hbm.1, ...), custom_call_target="tpu_custom_call" | custom-call | tf_op jit(solution)/shard_map/pallas_call | solution.py:185
  5.5 0.0 copy-start
  5.5 0.0 copy-start.1
  5.6 204.7 %all_to_all.10 = bf16[128,8,2048]{2,1,0:T(8,128)(2,1)S(1)} all-to-all(bf16[128,8,2048]{2,1,0:T(8,128)(2,1)} %bitcast.26), channel_id=1, replica_groups=mesh['dp'=4,'expert'=128] {'expert'}, dimensions={0} | all-to-all | bytes 8388608 | tf_op jit(solution)/shard_map/all_to_all | solution.py:204
  210.3 0.0 copy-start.2
  210.3 0.0 copy-start.3
  210.3 0.0 copy-start.4
  210.3 0.0 copy-done
  210.3 0.0 copy-done.1
  210.3 4.6 %shard_map.104 = (bf16[3072,128]{1,0:T(8,128)(2,1)S(1)}, bf16[3072,128]{1,0:T(8,128)(2,1)S(1)}, bf16[3072,128]{1,0:T(8,128)(2,1)S(1)}, bf16[3072,128]{1,0:T(8,128)(2,1)S(1)}, f32[128,128]{1,0:T(8,128)S(1)}) custom-call(s32[1]{0:T(128)} %bitcast.me_ref, bf16[1024,2048]{1,0:T(8,128)(2,1)S(1)} %bitcast.17, bf16[2048,384]{1,0:T(8,128)(2,1)S(1)} %bitcast.18, ...), custom_call_target="tpu_custom_call" | custom-call | tf_op jit(solution)/shard_map/pallas_call | solution.py:209
  214.8 3.2 %collective-permute-start = (bf16[3072,128]{1,0:T(8,128)(2,1)S(1)}, bf16[3072,128]{1,0:T(8,128)(2,1)S(1)}, u32[]{:S(2)}, u32[]{:S(2)}) collective-permute-start(bf16[3072,128]{1,0:T(8,128)(2,1)S(1)} %get-tuple-element.14), channel_id=1, source_target_pairs={{0,128},{128,256},{256,384},{384,0},{1,129},{129,257},{257,385},{3... | collective-permute-start | bytes 2359304 | tf_op jit(solution)/shard_map/ppermute | solution.py:224
  218.0 4.4 %collective-permute-start.1 = (bf16[3072,128]{1,0:T(8,128)(2,1)S(1)}, bf16[3072,128]{1,0:T(8,128)(2,1)S(1)}, u32[]{:S(2)}, u32[]{:S(2)}) collective-permute-start(bf16[3072,128]{1,0:T(8,128)(2,1)S(1)} %get-tuple-element.15), channel_id=1, source_target_pairs={{0,256},{128,384},{256,0},{384,128},{1,257},{129,385},{257,1},{385... | collective-permute-start | bytes 2359304 | tf_op jit(solution)/shard_map/ppermute | solution.py:224
  222.4 3.0 %collective-permute-start.2 = (bf16[3072,128]{1,0:T(8,128)(2,1)S(1)}, bf16[3072,128]{1,0:T(8,128)(2,1)S(1)}, u32[]{:S(2)}, u32[]{:S(2)}) collective-permute-start(bf16[3072,128]{1,0:T(8,128)(2,1)S(1)} %get-tuple-element.16), channel_id=1, source_target_pairs={{0,384},{128,0},{256,128},{384,256},{1,385},{129,1},{257,129},{385... | collective-permute-start | bytes 2359304 | tf_op jit(solution)/shard_map/ppermute | solution.py:224
  225.4 28.7 %all_to_all.11 = f32[128,1,128]{2,1,0:T(1,128)S(1)} all-to-all(f32[128,1,128]{2,1,0:T(1,128)S(1)} %bitcast.21), channel_id=1, replica_groups=mesh['dp'=4,'expert'=128] {'expert'}, dimensions={0} | all-to-all | bytes 131072 | tf_op jit(solution)/shard_map/all_to_all | solution.py:237
  254.1 0.0 copy-done.2
  254.1 0.0 copy-done.3
  254.1 0.0 copy-done.4
  254.1 0.7 shard_map.106
  254.8 0.0 collective-permute-done.ahead_ref
  254.8 0.0 collective-permute-done.1.far_ref
  254.8 0.9 collective-permute-done.2.behind_ref
  255.7 1.2 shard_map.105
Async XLA Ops:
  5.5 204.7 %copy-start = (bf16[1,2048,384]{2,1,0:T(8,128)(2,1)S(1)}, bf16[1,2048,384]{2,1,0:T(8,128)(2,1)}, u32[]{:S(2)}) copy-start(bf16[1,2048,384]{2,1,0:T(8,128)(2,1)} %param.14) | copy-start | bytes 4718596
  5.5 204.7 %copy-start.1 = (bf16[1,384,2048]{2,1,0:T(8,128)(2,1)S(1)}, bf16[1,384,2048]{2,1,0:T(8,128)(2,1)}, u32[]{:S(2)}) copy-start(bf16[1,384,2048]{2,1,0:T(8,128)(2,1)} %param.15) | copy-start | bytes 4718596
  210.3 43.8 %copy-start.2 = (f32[128,128]{1,0:T(8,128)S(1)}, f32[128,128]{1,0:T(8,128)}, u32[]{:S(2)}) copy-start(f32[128,128]{1,0:T(8,128)} %get-tuple-element.20.code_ref) | copy-start | bytes 196612
  210.3 43.8 %copy-start.3 = (s32[128,4]{0,1:T(4,128)S(1)}, s32[128,4]{0,1:T(4,128)}, u32[]{:S(2)}) copy-start(s32[128,4]{0,1:T(4,128)} %param.11) | copy-start | bytes 6148
  210.3 43.8 %copy-start.4 = (bf16[128,4]{0,1:T(4,128)(2,1)S(1)}, bf16[128,4]{0,1:T(4,128)(2,1)}, u32[]{:S(2)}) copy-start(bf16[128,4]{0,1:T(4,128)(2,1)} %param.10) | copy-start | bytes 3076
  214.8 40.0 %collective-permute-start = (bf16[3072,128]{1,0:T(8,128)(2,1)S(1)}, bf16[3072,128]{1,0:T(8,128)(2,1)S(1)}, u32[]{:S(2)}, u32[]{:S(2)}) collective-permute-start(bf16[3072,128]{1,0:T(8,128)(2,1)S(1)} %get-tuple-element.14), channel_id=1, source_target_pairs={{0,128},{128,256},{256,384},{384,0},{1,129},{129,257},{257,385},{3... | collective-permute-start | bytes 2359304 | tf_op jit(solution)/shard_map/ppermute | solution.py:224
  218.0 36.8 %collective-permute-start.1 = (bf16[3072,128]{1,0:T(8,128)(2,1)S(1)}, bf16[3072,128]{1,0:T(8,128)(2,1)S(1)}, u32[]{:S(2)}, u32[]{:S(2)}) collective-permute-start(bf16[3072,128]{1,0:T(8,128)(2,1)S(1)} %get-tuple-element.15), channel_id=1, source_target_pairs={{0,256},{128,384},{256,0},{384,128},{1,257},{129,385},{257,1},{385... | collective-permute-start | bytes 2359304 | tf_op jit(solution)/shard_map/ppermute | solution.py:224
  222.4 33.4 %collective-permute-start.2 = (bf16[3072,128]{1,0:T(8,128)(2,1)S(1)}, bf16[3072,128]{1,0:T(8,128)(2,1)S(1)}, u32[]{:S(2)}, u32[]{:S(2)}) collective-permute-start(bf16[3072,128]{1,0:T(8,128)(2,1)S(1)} %get-tuple-element.16), channel_id=1, source_target_pairs={{0,384},{128,0},{256,128},{384,256},{1,385},{129,1},{257,129},{385... | collective-permute-start | bytes 2359304 | tf_op jit(solution)/shard_map/ppermute | solution.py:224

commit v9 on v8

--- a/solution.py
+++ b/solution.py
@@ -131,11 +131,11 @@
         dot_ref[r * groups : (r + 1) * groups, :] = spread
         dot_ref[(r + STEPS) * groups : (r + STEPS + 1) * groups, :] = pltpu.roll(spread, LANES - SLOTS, 1)
     parts = width * pre_ref.shape[1] * 2 // (own_ref.shape[0] * LANES)
-    for shift, out_ref in ((1, ahead_ref), (2, far_ref), (3, behind_ref), (0, own_ref)):
+    for shift, out_ref in ((2, far_ref), (3, behind_ref), (1, ahead_ref), (0, own_ref)):
         write_piece(lax.rem(me_ref[0] + shift, parts), x_ref, s_ref, hid_ref, pre_ref, out_ref)
 
 
-def add_pieces(own_ref, ahead_ref, far_ref, behind_ref, up_ref, down_ref):
+def add_pieces(own_ref, far_ref, behind_ref, ahead_ref, up_ref, down_ref):
     refs = (own_ref, far_ref, ahead_ref, behind_ref)
     wide, tall = up_ref.shape
     base = wide * tall // LANES
@@ -223,7 +223,7 @@
     def shift(block, distance):
         return lax.ppermute(block, "dp", [(i, (i + distance) % groups) for i in range(groups)])
 
-    ahead, far, behind = shift(ahead, 1), shift(far, 2), shift(behind, 3)
+    far, behind, ahead = shift(far, 2), shift(behind, 3), shift(ahead, 1)
     summed_up, summed_down = pl.pallas_call(
         add_pieces,
         out_shape=(
@@ -233,7 +233,7 @@
         in_specs=[VMEM] * 4,
         out_specs=(VMEM,) * 2,
         compiler_params=pltpu.CompilerParams(vmem_limit_bytes=12 << 20),
-    )(own, ahead, far, behind)
+    )(own, far, behind, ahead)
     back = lax.all_to_all(
         dots.reshape(experts, 1, LANES), "expert", split_axis=0, concat_axis=0, tiled=True
     )

time: 262 us -> 259 us (0.989)
  no operation moved by 1% of the time
where the time goes in v9:
time: 259 us; the launch traced here: 256 us
  blocking collectives  233 us (90%)
  Pallas kernels  11.4 us (4%)
  starting transfers between devices  9.94 us (4%)
    all_to_all x1, blocking collectives, shards(): lax.all_to_all(sent.reshape(experts, CHUNK, width), 'expert', split_axis=...  205 us
    all_to_all x1, blocking collectives, shards(): lax.all_to_all(dots.reshape(experts, 1, LANES), 'expert', split_axis=0, c...  28.7 us
    ppermute x3, starting transfers between devices, shift(): lax.ppermute(block, 'dp', [(i, (i + distance) % groups) for i in range(gr...  9.94 us
  transfers between devices with their start and end apart: 3, of which 1 were waited for; matrix products, arithmetic and copies ran while one was open for 0% of the time, Pallas kernels for 0%

profile of v9, /device:TPU:1, one launch (start us, length us, event | category | flops | bytes accessed | tf_op | source)
XLA Modules:
  0.0 255.7 jit_solution(1604879509131696508)
XLA Ops:
  0.6 4.9 %shard_map.103 = (bf16[1024,2048]{1,0:T(8,128)(2,1)}, f32[128,128]{1,0:T(8,128)}) custom-call(s32[1]{0:T(128)} %bitcast.me_ref, s32[1]{0:T(128)} %bitcast.1.odd_ref, s32[4,128]{1,0:T(4,128)} %bitcast.22, bf16[4,128]{1,0:T(4,128)(2,1)} %bitcast.24, s32[1,128]{1,0:T(1,128)} %bitcast.28, s32[1,128]{1,0:T(1,128)} %bitcast.29, bf16[128,2048]{1,0:T(8,128)(2,1)} %x_hbm.1, ...), custom_call_target="tpu_custom_call" | custom-call | tf_op jit(solution)/shard_map/pallas_call | solution.py:185
  5.5 0.0 copy-start
  5.5 0.0 copy-start.1
  5.6 204.7 %all_to_all.10 = bf16[128,8,2048]{2,1,0:T(8,128)(2,1)S(1)} all-to-all(bf16[128,8,2048]{2,1,0:T(8,128)(2,1)} %bitcast.26), channel_id=1, replica_groups=mesh['dp'=4,'expert'=128] {'expert'}, dimensions={0} | all-to-all | bytes 8388608 | tf_op jit(solution)/shard_map/all_to_all | solution.py:204
  210.3 0.0 copy-start.2
  210.3 0.0 copy-start.3
  210.3 0.0 copy-start.4
  210.3 0.0 copy-done
  210.3 0.0 copy-done.1
  210.3 4.6 %shard_map.104 = (bf16[3072,128]{1,0:T(8,128)(2,1)S(1)}, bf16[3072,128]{1,0:T(8,128)(2,1)S(1)}, bf16[3072,128]{1,0:T(8,128)(2,1)S(1)}, bf16[3072,128]{1,0:T(8,128)(2,1)S(1)}, f32[128,128]{1,0:T(8,128)S(1)}) custom-call(s32[1]{0:T(128)} %bitcast.me_ref, bf16[1024,2048]{1,0:T(8,128)(2,1)S(1)} %bitcast.17, bf16[2048,384]{1,0:T(8,128)(2,1)S(1)} %bitcast.18, ...), custom_call_target="tpu_custom_call" | custom-call | tf_op jit(solution)/shard_map/pallas_call | solution.py:209
  214.9 4.7 %collective-permute-start = (bf16[3072,128]{1,0:T(8,128)(2,1)S(1)}, bf16[3072,128]{1,0:T(8,128)(2,1)S(1)}, u32[]{:S(2)}, u32[]{:S(2)}) collective-permute-start(bf16[3072,128]{1,0:T(8,128)(2,1)S(1)} %get-tuple-element.14), channel_id=1, source_target_pairs={{0,256},{128,384},{256,0},{384,128},{1,257},{129,385},{257,1},{385... | collective-permute-start | bytes 2359304 | tf_op jit(solution)/shard_map/ppermute | solution.py:224
  219.5 2.7 %collective-permute-start.1 = (bf16[3072,128]{1,0:T(8,128)(2,1)S(1)}, bf16[3072,128]{1,0:T(8,128)(2,1)S(1)}, u32[]{:S(2)}, u32[]{:S(2)}) collective-permute-start(bf16[3072,128]{1,0:T(8,128)(2,1)S(1)} %get-tuple-element.15), channel_id=1, source_target_pairs={{0,384},{128,0},{256,128},{384,256},{1,385},{129,1},{257,129},{385... | collective-permute-start | bytes 2359304 | tf_op jit(solution)/shard_map/ppermute | solution.py:224
  222.3 2.6 collective-permute-start.2
  224.8 28.7 %all_to_all.11 = f32[128,1,128]{2,1,0:T(1,128)S(1)} all-to-all(f32[128,1,128]{2,1,0:T(1,128)S(1)} %bitcast.21), channel_id=1, replica_groups=mesh['dp'=4,'expert'=128] {'expert'}, dimensions={0} | all-to-all | bytes 131072 | tf_op jit(solution)/shard_map/all_to_all | solution.py:237
  253.5 0.0 copy-done.2
  253.5 0.0 copy-done.3
  253.5 0.0 copy-done.4
  253.5 0.7 shard_map.106
  254.2 0.0 collective-permute-done.far_ref
  254.2 0.0 collective-permute-done.1.behind_ref
  254.2 0.3 collective-permute-done.2.ahead_ref
  254.5 1.2 shard_map.105
Async XLA Ops:
  5.5 204.7 %copy-start = (bf16[1,2048,384]{2,1,0:T(8,128)(2,1)S(1)}, bf16[1,2048,384]{2,1,0:T(8,128)(2,1)}, u32[]{:S(2)}) copy-start(bf16[1,2048,384]{2,1,0:T(8,128)(2,1)} %param.14) | copy-start | bytes 4718596
  5.5 204.7 %copy-start.1 = (bf16[1,384,2048]{2,1,0:T(8,128)(2,1)S(1)}, bf16[1,384,2048]{2,1,0:T(8,128)(2,1)}, u32[]{:S(2)}) copy-start(bf16[1,384,2048]{2,1,0:T(8,128)(2,1)} %param.15) | copy-start | bytes 4718596
  210.3 43.2 %copy-start.2 = (f32[128,128]{1,0:T(8,128)S(1)}, f32[128,128]{1,0:T(8,128)}, u32[]{:S(2)}) copy-start(f32[128,128]{1,0:T(8,128)} %get-tuple-element.20.code_ref) | copy-start | bytes 196612
  210.3 43.2 %copy-start.3 = (s32[128,4]{0,1:T(4,128)S(1)}, s32[128,4]{0,1:T(4,128)}, u32[]{:S(2)}) copy-start(s32[128,4]{0,1:T(4,128)} %param.11) | copy-start | bytes 6148
  210.3 43.2 %copy-start.4 = (bf16[128,4]{0,1:T(4,128)(2,1)S(1)}, bf16[128,4]{0,1:T(4,128)(2,1)}, u32[]{:S(2)}) copy-start(bf16[128,4]{0,1:T(4,128)(2,1)} %param.10) | copy-start | bytes 3076
  214.9 39.4 %collective-permute-start = (bf16[3072,128]{1,0:T(8,128)(2,1)S(1)}, bf16[3072,128]{1,0:T(8,128)(2,1)S(1)}, u32[]{:S(2)}, u32[]{:S(2)}) collective-permute-start(bf16[3072,128]{1,0:T(8,128)(2,1)S(1)} %get-tuple-element.14), channel_id=1, source_target_pairs={{0,256},{128,384},{256,0},{384,128},{1,257},{129,385},{257,1},{385... | collective-permute-start | bytes 2359304 | tf_op jit(solution)/shard_map/ppermute | solution.py:224
  219.5 34.7 %collective-permute-start.1 = (bf16[3072,128]{1,0:T(8,128)(2,1)S(1)}, bf16[3072,128]{1,0:T(8,128)(2,1)S(1)}, u32[]{:S(2)}, u32[]{:S(2)}) collective-permute-start(bf16[3072,128]{1,0:T(8,128)(2,1)S(1)} %get-tuple-element.15), channel_id=1, source_target_pairs={{0,384},{128,0},{256,128},{384,256},{1,385},{129,1},{257,129},{385... | collective-permute-start | bytes 2359304 | tf_op jit(solution)/shard_map/ppermute | solution.py:224
  222.3 32.3 %collective-permute-start.2 = (bf16[3072,128]{1,0:T(8,128)(2,1)S(1)}, bf16[3072,128]{1,0:T(8,128)(2,1)S(1)}, u32[]{:S(2)}, u32[]{:S(2)}) collective-permute-start(bf16[3072,128]{1,0:T(8,128)(2,1)S(1)} %get-tuple-element.16), channel_id=1, source_target_pairs={{0,128},{128,256},{256,384},{384,0},{1,129},{129,257},{257,385},{3... | collective-permute-start | bytes 2359304 | tf_op jit(solution)/shard_map/ppermute | solution.py:224
